TPU v7x, 256 devices: a whole 4x4x8 slice. The times are simulated.
256 devices in a mesh: rows: 16 (over x, y), cols: 16 (over z, core).
Axes of the slice: x: 4, y: 4, z: 8, core: 2. Of those that a mesh axis runs over, the one named last changes fastest.
Arguments:
- latent1: bfloat16 [256, 1024, 320], P('rows', 'cols'), may hold values from -15 to 15, as said below
- norm1a_g: float32 [320], replicated, may hold values from 0.25 to 1.75
- norm1a_b: float32 [320], replicated, may hold values from -3 to 3
- conv1a_w: bfloat16 [3, 3, 320, 320], replicated, may hold values from -0.109375 to 0.109375
- norm1b_g: float32 [320], replicated, may hold values from 0.25 to 1.75
- norm1b_b: float32 [320], replicated, may hold values from -3 to 3
- conv1b_w: bfloat16 [3, 3, 320, 320], replicated, may hold values from -0.109375 to 0.109375
- conv1b_b: float32 [320], replicated, may hold values from -3 to 3
- feat3: bfloat16 [64, 256, 1280], P('rows', 'cols'), may hold values from -15 to 15, as said below
- adapter3: bfloat16 [64, 256, 1280], P('rows', 'cols'), may hold values from -15 to 15, as said below
- norm3a_g: float32 [1280], replicated, may hold values from 0.25 to 1.75
- norm3a_b: float32 [1280], replicated, may hold values from -3 to 3
- conv3a_w: bfloat16 [3, 3, 1280, 1280], P(None, None, None, 'cols'), may hold values from -0.0546875 to 0.0546875
- norm3b_g: float32 [1280], P('cols'), may hold values from 0.25 to 1.75
- norm3b_b: float32 [1280], P('cols'), may hold values from -3 to 3
- conv3b_w: bfloat16 [3, 3, 1280, 1280], P(None, None, None, 'cols'), may hold values from -0.0546875 to 0.0546875
- conv3b_b: float32 [1280], P('cols'), may hold values from -3 to 3
Outputs:
- out1: bfloat16 [256, 1024, 320], P('rows', 'cols')
- out3: bfloat16 [64, 256, 1280], P('rows', None, 'cols')
Inputs may be any that keep to these rules, and one draw needn't show every extreme that they name: `latent1`: real values. `feat3`: real values. `adapter3`: real values.
All inputs are finite; a program needn't handle non-finite values.
Results may differ from a plain program's by a relative error of at most 0.0052.
Values may be sent and summed in bfloat16 or wider, within the bound.
A program may use at most 128 MiB of HBM per device.

v0:
```python
import functools

import jax
import jax.numpy as jnp
from jax import lax
from jax.experimental import pallas as pl
from jax.experimental.pallas import tpu as pltpu
from jax.sharding import PartitionSpec as P

MESH = pl.DeviceIdType.MESH
F32 = jnp.float32
BF16 = jnp.bfloat16
EPS = 1e-05
R, C = 16, 16
Z = 8
C1, C3, OC = 320, 1280, 80
H1, W1 = 16, 64
H3, W3 = 4, 256
WP = 80
NT = (((1,), (1,)), ((), ()))
COUNT1 = float(R * H1 * C * W1 * (C1 // 32))
COUNT3 = float(R * H3 * W3 * (C3 // 32))


def iota(shape, dim):
    return lax.broadcasted_iota(jnp.int32, shape, dim)


def group_matrix(chans, width, offset):
    chan = iota((chans, 128), 0)
    first = (iota((chans, 128), 1) - offset) * width
    return jnp.where((chan >= first) & (chan < first + width), 1.0, 0.0).astype(F32)


def exact_dot(a, b, dims=(((1,), (0,)), ((), ()))):
    return lax.dot_general(a, b, dims, precision=lax.Precision.HIGHEST, preferred_element_type=F32)


def halves(value):
    return value + value * jnp.tanh(value)


def kernel(
    lat_h, g1a, b1a, w1a_h, g1b, b1b, w1b_h, c1b, feat_h, adap_h, g3a, b3a, w3a_h, g3b, b3b, w3b_h, c3b,
    out1_h, out3_h,
    lat, top, bottom, pack, side, act, hid, w1a, w1b, w3a, w3b, feat, adap, gat1, act3, gat2, prod,
    edge_s, edge_r, hid3, res, o1, o3, st_a1, st_a2, st_b1, st_b2, st_c,
    local_sem, ar_send, ar_recv, ring_send, ring_recv, mate_send, mate_recv, own_send,
    halo_send, halo_recv, edge_send, edge_recv,
):
    row = lax.axis_index("rows")
    col = lax.axis_index("cols")
    z = col // 2
    core = col % 2
    up = (row + R - 1) % R
    down = (row + 1) % R
    left = (col + C - 1) % C
    right = (col + 1) % C
    mate = z * 2 + (1 - core)

    def local(src, dst, index):
        return pltpu.make_async_copy(src, dst, local_sem.at[index])

    loads = {
        "feat": local(feat_h, feat, 0),
        "adap": local(adap_h, adap, 1),
        "lat": local(lat_h, lat, 2),
        "w1a": local(w1a_h, w1a, 3),
        "w3a": local(w3a_h, w3a, 4),
        "w1b": local(w1b_h, w1b, 5),
        "w3b": local(w3b_h, w3b, 6),
    }
    for copy in loads.values():
        copy.start()

    barrier = pltpu.get_barrier_semaphore()
    for step in range(1, R):
        pl.semaphore_signal(barrier, inc=1, device_id={"rows": (row + step) % R}, device_id_type=MESH)
    for step in range(1, C):
        pl.semaphore_signal(barrier, inc=1, device_id={"cols": (col + step) % C}, device_id_type=MESH)

    def spread(buf, axis, index):
        me = row if axis == "rows" else col

        def send(step, carry):
            pltpu.make_async_remote_copy(
                src_ref=buf.at[0],
                dst_ref=buf.at[step],
                send_sem=ar_send.at[index],
                recv_sem=ar_recv.at[index],
                device_id={axis: (me + step) % 16},
                device_id_type=MESH,
            ).start()
            return carry

        lax.fori_loop(1, 16, send, 0)

    def collect(buf, axis, index):
        rest = pltpu.make_async_remote_copy(
            src_ref=buf.at[pl.ds(1, 15)],
            dst_ref=buf.at[pl.ds(1, 15)],
            send_sem=ar_send.at[index],
            recv_sem=ar_recv.at[index],
            device_id={axis: ((row if axis == "rows" else col) + 1) % 16},
            device_id_type=MESH,
        )
        rest.wait_recv()
        rest.wait_send()
        return jnp.sum(buf[...], axis=0)

    def origin(direction, hop):
        return (z + Z - hop) % Z if direction == 0 else (z + hop) % Z

    def chunk(gat, slot, half):
        return gat.at[slot, pl.ds(2 * half, 2)]

    def ring_copy(which, gat, direction, hop, half):
        slot = 2 * origin(direction, hop - 1) + core
        target = 2 * ((z + 1) % Z if direction == 0 else (z + Z - 1) % Z) + core
        return pltpu.make_async_remote_copy(
            src_ref=chunk(gat, slot, half),
            dst_ref=chunk(gat, slot, half),
            send_sem=ring_send.at[which, direction, hop - 1, half],
            recv_sem=ring_recv.at[which, direction, hop - 1, half],
            device_id={"cols": target},
            device_id_type=MESH,
        )

    def ring_wait(which, gat, direction, hop, half):
        slot = 2 * origin(direction, hop) + core
        target = 2 * ((z + 1) % Z if direction == 0 else (z + Z - 1) % Z) + core
        pltpu.make_async_remote_copy(
            src_ref=chunk(gat, slot, half),
            dst_ref=chunk(gat, slot, half),
            send_sem=ring_send.at[which, direction, hop - 1, half],
            recv_sem=ring_recv.at[which, direction, hop - 1, half],
            device_id={"cols": target},
            device_id_type=MESH,
        ).wait_recv()

    def mate_copy(which, gat, direction, hop, half):
        slot = 2 * origin(direction, hop) + core
        return pltpu.make_async_remote_copy(
            src_ref=chunk(gat, slot, half),
            dst_ref=chunk(gat, slot, half),
            send_sem=mate_send.at[which, direction, hop, half],
            recv_sem=mate_recv.at[which, direction, hop, half],
            device_id={"cols": mate},
            device_id_type=MESH,
        )

    def mate_wait(which, gat, direction, hop, half):
        slot = 2 * origin(direction, hop) + (1 - core)
        pltpu.make_async_remote_copy(
            src_ref=chunk(gat, slot, half),
            dst_ref=chunk(gat, slot, half),
            send_sem=mate_send.at[which, direction, hop, half],
            recv_sem=mate_recv.at[which, direction, hop, half],
            device_id={"cols": mate},
            device_id_type=MESH,
        ).wait_recv()

    def arrivals(hop):
        if hop == 4:
            return [(0, 0), (1, 1)]
        return [(direction, half) for half in range(2) for direction in range(2)]

    sends = []

    def go(copy):
        copy.start()
        sends.append(copy)

    def ring_start(which, gat):
        for half in range(2):
            for direction in range(2):
                go(ring_copy(which, gat, direction, 1, half))
        for half in range(2):
            go(mate_copy(which, gat, 0, 0, half))

    def ring_step(which, gat, hop):
        for direction, half in arrivals(hop):
            ring_wait(which, gat, direction, hop, half)
            if (direction, half) in (arrivals(hop + 1) if hop < 4 else []):
                go(ring_copy(which, gat, direction, hop + 1, half))
            go(mate_copy(which, gat, direction, hop, half))

    def mate_step(which, gat, hop):
        if hop == 0:
            for half in range(2):
                mate_wait(which, gat, 0, 0, half)
        else:
            for direction, half in arrivals(hop):
                mate_wait(which, gat, direction, hop, half)

    loads["feat"].wait()
    loads["adap"].wait()
    js = jnp.zeros((8, C3), F32)
    jq = jnp.zeros((8, C3), F32)
    for i in range(H3):
        value = (feat[i].astype(F32) + adap[i].astype(F32)).astype(BF16)
        gat1[col, i] = value
        value = value.astype(F32).reshape(2, 8, C3)
        js = js + jnp.sum(value, axis=0)
        jq = jq + jnp.sum(value * value, axis=0)

    pl.semaphore_wait(barrier, R - 1 + C - 1)
    ring_start(0, gat1)

    loads["lat"].wait()

    def halo_copy(src, dst, index, target):
        return pltpu.make_async_remote_copy(
            src_ref=src,
            dst_ref=dst,
            send_sem=halo_send.at[index],
            recv_sem=halo_recv.at[index],
            device_id=target,
            device_id_type=MESH,
        )

    to_down = halo_copy(lat.at[pl.ds(H1 - 2, 2)], top, 0, {"rows": down})
    to_up = halo_copy(lat.at[pl.ds(0, 2)], bottom, 1, {"rows": up})
    to_down.start()
    to_up.start()

    ls = jnp.zeros((8, C1), F32)
    lq = jnp.zeros((8, C1), F32)
    for i in range(H1):
        value = lat[i].astype(F32).reshape(8, 8, C1)
        ls = ls + jnp.sum(value, axis=0)
        lq = lq + jnp.sum(value * value, axis=0)
    st_a1[0] = (
        exact_dot(ls, group_matrix(C1, 10, 0))
        + exact_dot(lq, group_matrix(C1, 10, 32))
        + exact_dot(js, group_matrix(C3, 40, 64))
        + exact_dot(jq, group_matrix(C3, 40, 96))
    )
    spread(st_a1, "rows", 0)

    to_down.wait()
    to_up.wait()

    def extended_row(i):
        if i < 2:
            return top[i]
        if i < H1 + 2:
            return lat[i - 2]
        return bottom[i - H1 - 2]

    for block in range(3):
        rows_here = [i for i in range(8 * block, 8 * block + 8) if i < H1 + 4]
        tiles = [jnp.zeros((8, C1), F32) for _ in range(4)]
        for i in rows_here:
            value = extended_row(i)
            first = value[0:16].astype(F32)
            last = value[48:64].astype(F32)
            here = iota((8, C1), 0) == i - 8 * block
            for j, piece in enumerate((last[14:15], last[15:16], first[0:1], first[1:2])):
                tiles[j] = jnp.where(here, jnp.broadcast_to(piece, (8, C1)), tiles[j])
        for j in range(4):
            pack[j // 2, j % 2, pl.ds(8 * block, 8), :] = tiles[j]
    to_right = halo_copy(pack.at[0], side.at[0], 2, {"cols": right})
    to_left = halo_copy(pack.at[1], side.at[1], 3, {"cols": left})
    to_right.start()
    to_left.start()

    st_a2[0] = collect(st_a1, "rows", 0)
    spread(st_a2, "cols", 1)
    ring_step(0, gat1, 1)

    def group_rates(total):
        total = jnp.sum(total, axis=0, keepdims=True)
        total = jnp.broadcast_to(total, (8, 128))
        lane = iota((8, 128), 1)
        count = jnp.where(lane < 64, COUNT1, COUNT3)
        squares = pltpu.roll(total, 96, 1)
        mean = total / count
        spread_of = squares / count - mean * mean
        live = (lane < 32) | ((lane >= 64) & (lane < 96))
        inverse = lax.rsqrt(jnp.where(live, spread_of, 1.0) + EPS)
        return jnp.where(live, mean, 0.0), jnp.where(live, inverse, 0.0)

    def channel_rates(rates, matrix, gain, shift):
        mean, inverse = (exact_dot(x, matrix, NT)[0:1] for x in rates)
        scale = inverse * gain
        return 0.5 * scale, 0.5 * (shift - mean * scale)

    rates = group_rates(collect(st_a2, "cols", 1))
    scale1, shift1 = channel_rates(rates, group_matrix(C1, 10, 0), g1a[...], b1a[...])
    scale3, shift3 = channel_rates(rates, group_matrix(C3, 40, 64), g3a[...], b3a[...])

    def put_row(i, value, live):
        value = jnp.where(live, halves(value), 0.0)
        act[i, :, 0:C1] = pltpu.roll(value, 1, 0).astype(BF16)
        act[i, :, C1 : 2 * C1] = value.astype(BF16)
        act[i, :, 2 * C1 : 3 * C1] = pltpu.roll(value, WP - 1, 0).astype(BF16)

    place = iota((WP, C1), 0)

    to_right.wait()
    to_left.wait()
    slab_place = iota((16, C1), 0)
    wide_ok = (place < W1) | ((place < W1 + 2) & (col < C - 1)) | ((place >= WP - 2) & (col > 0))

    def act1_rows(first, last):
        for i in range(first, last):
            slab = jnp.zeros((16, C1), F32)
            base = 8 * (i // 8)
            for target, which, j in ((0, 1, 0), (1, 1, 1), (14, 0, 0), (15, 0, 1)):
                piece = side[which, j, pl.ds(base, 8), :][i - base : i - base + 1]
                slab = jnp.where(slab_place == target, jnp.broadcast_to(piece, (16, C1)), slab)
            value = jnp.concatenate([extended_row(i).astype(F32), slab], axis=0)
            live = wide_ok
            if i < 2:
                live = live & (row > 0)
            if i >= H1 + 2:
                live = live & (row < R - 1)
            put_row(i, value * scale1 + shift1, live)

    act1_rows(0, 10)
    ring_step(0, gat1, 2)
    act1_rows(10, 20)

    def conv1(weights, first, count, width):
        total = None
        for dy in range(3):
            block = act[pl.ds(first + dy, count), 0:width, :].reshape(count * width, 3 * C1)
            part = jnp.dot(block, weights[dy], preferred_element_type=F32)
            total = part if total is None else total + part
        return total.reshape(count, width, C1)

    def norm3(slot):
        for i in range(H3):
            value = gat1[slot, i].astype(F32) * scale3 + shift3
            act3[slot, i] = halves(value).astype(BF16)

    def norm3_hop(hop):
        mate_step(0, gat1, hop)
        for direction in range(1 if hop in (0, 4) else 2):
            for k in range(2):
                norm3(2 * origin(direction, hop) + k)

    loads["w1a"].wait()
    hid[pl.ds(0, 6)] = conv1(w1a, 0, 6, WP)
    ring_step(0, gat1, 3)
    hid[pl.ds(6, 6)] = conv1(w1a, 6, 6, WP)
    norm3_hop(0)
    norm3_hop(1)
    ring_step(0, gat1, 4)
    hid[pl.ds(12, 6)] = conv1(w1a, 12, 6, WP)

    hs = jnp.zeros((8, C1), F32)
    hq = jnp.zeros((8, C1), F32)
    for i in range(H1):
        value = hid[i + 1, 0:W1, :].reshape(8, 8, C1)
        hs = hs + jnp.sum(value, axis=0)
        hq = hq + jnp.sum(value * value, axis=0)
    st_b1[0] = exact_dot(hs, group_matrix(C1, 10, 0)) + exact_dot(hq, group_matrix(C1, 10, 32))
    spread(st_b1, "rows", 2)

    norm3_hop(2)
    norm3_hop(3)
    norm3_hop(4)

    def taps(weights, source, dims):
        def one(i, carry):
            prod[i] = lax.dot_general(weights[...], source(i), dims, preferred_element_type=F32)
            return carry

        lax.fori_loop(0, H3, one, 0)

    lane3 = iota((OC, W3), 1)

    def combine(target):
        columns = []
        for dx in range(3):
            total = None
            for dy in range(3):
                i = target + dy - 1
                if 0 <= i < H3:
                    part = prod[i, pl.ds((3 * dy + dx) * OC, OC), :]
                    total = part if total is None else total + part
            columns.append(total)
        before = jnp.where(lane3 == 0, 0.0, pltpu.roll(columns[0], 1, 1))
        after = jnp.where(lane3 == W3 - 1, 0.0, pltpu.roll(columns[2], W3 - 1, 1))
        return before + columns[1] + after

    def edge_copies(which):
        return [
            pltpu.make_async_remote_copy(
                src_ref=edge_s.at[which, j],
                dst_ref=edge_r.at[which, j],
                send_sem=edge_send.at[which, j],
                recv_sem=edge_recv.at[which, j],
                device_id={"rows": target},
                device_id_type=MESH,
            )
            for j, target in ((0, down), (1, up))
        ]

    def edges_out(which):
        edge_s[which, 0] = combine(H3)
        edge_s[which, 1] = combine(-1)
        copies = edge_copies(which)
        for copy in copies:
            copy.start()
        return copies

    def edges_in(which):
        low = jnp.where(row > 0, edge_r[which, 0], 0.0)
        high = jnp.where(row < R - 1, edge_r[which, 1], 0.0)
        return low, high

    loads["w3a"].wait()
    taps(w3a, lambda i: act3[:, i].reshape(W3, C3), NT)
    copies = edges_out(0)
    st_b2[0] = collect(st_b1, "rows", 2)
    spread(st_b2, "cols", 3)
    for i in range(H3):
        hid3[i] = combine(i)
    for copy in copies:
        copy.wait()
    low, high = edges_in(0)
    hid3[0] = hid3[0] + low
    hid3[H3 - 1] = hid3[H3 - 1] + high

    fs = jnp.zeros((OC, W3), F32)
    fq = jnp.zeros((OC, W3), F32)
    for i in range(H3):
        value = hid3[i]
        fs = fs + value
        fq = fq + value * value
    fs = jnp.sum(fs, axis=1, keepdims=True)
    fq = jnp.sum(fq, axis=1, keepdims=True)
    lane = iota((OC, 128), 1)
    second = iota((OC, 128), 0) >= OC // 2
    group = jnp.where(second, 1, 0)
    laid = jnp.where(lane == group, fs, 0.0) + jnp.where(lane == group + 2, fq, 0.0)
    st_c[0] = jnp.sum(laid.reshape(OC // 8, 8, 128), axis=0)
    spread(st_c, "rows", 4)

    rates = group_rates(collect(st_b2, "cols", 3))
    scale2, shift2 = channel_rates(rates, group_matrix(C1, 10, 0), g1b[...], b1b[...])
    near_ok = (place < W1) | ((place == W1) & (col < C - 1)) | ((place == WP - 1) & (col > 0))

    def act2_rows(first, last):
        for i in range(first, last):
            live = near_ok
            if i == 0:
                live = live & (row > 0)
            if i == H1 + 1:
                live = live & (row < R - 1)
            put_row(i, hid[i] * scale2 + shift2, live)

    act2_rows(0, 6)

    total = jnp.sum(collect(st_c, "rows", 4), axis=0, keepdims=True)
    total = jnp.broadcast_to(total, (OC, 128)) / COUNT3
    mean = jnp.sum(jnp.where(lane == group, total, 0.0), axis=1, keepdims=True)
    square = jnp.sum(jnp.where(lane == group + 2, total, 0.0), axis=1, keepdims=True)
    inverse = lax.rsqrt(square - mean * mean + EPS)

    def upright(ref):
        eye = iota((OC, OC), 0) == iota((OC, OC), 1)
        return jnp.sum(jnp.where(eye, jnp.broadcast_to(ref[...], (OC, OC)), 0.0), axis=1, keepdims=True)

    scale4 = inverse * upright(g3b)
    shift4 = 0.5 * (upright(b3b) - mean * scale4)
    scale4 = 0.5 * scale4
    for i in range(H3):
        gat2[col, i] = halves(hid3[i] * scale4 + shift4).astype(BF16)
    ring_start(1, gat2)

    act2_rows(6, 18)
    loads["w1b"].wait()

    def out1_rows(first, count):
        value = conv1(w1b, first, count, W1) + c1b[...].reshape(1, 1, C1)
        o1[pl.ds(first, count)] = (lat[pl.ds(first, count)].astype(F32) + value).astype(BF16)

    ring_step(1, gat2, 1)
    out1_rows(0, 8)
    ring_step(1, gat2, 2)
    out1_rows(8, 8)
    write1 = local(o1, out1_h, 7)
    write1.start()
    ring_step(1, gat2, 3)

    pick = jnp.where(iota((OC, C3), 1) == iota((OC, C3), 0) + col * OC, 1.0, 0.0).astype(BF16)

    def residual(i, carry):
        res[i] = lax.dot_general(pick, gat1[:, i].reshape(W3, C3), NT, preferred_element_type=F32)
        return carry

    lax.fori_loop(0, H3, residual, 0)
    bias3 = upright(c3b)
    ring_step(1, gat2, 4)
    for hop in range(5):
        mate_step(1, gat2, hop)

    loads["w3b"].wait()
    taps(w3b, lambda i: gat2[:, i].reshape(C3, W3), (((1,), (0,)), ((), ())))
    copies = edges_out(1)
    for i in range(H3):
        res[i] = res[i] + combine(i) + bias3
    for copy in copies:
        copy.wait()
    low, high = edges_in(1)
    res[0] = res[0] + low
    res[H3 - 1] = res[H3 - 1] + high
    for i in range(H3):
        o3[i] = res[i].astype(BF16)
    write3 = local(o3, out3_h, 8)
    write3.start()
    for copy in sends:
        copy.wait_send()
    write1.wait()
    write3.wait()


def body(
    latent1, norm1a_g, norm1a_b, conv1a_w, norm1b_g, norm1b_b, conv1b_w, conv1b_b,
    feat3, adapter3, norm3a_g, norm3a_b, conv3a_w, norm3b_g, norm3b_b, conv3b_w, conv3b_b,
):
    def flat(x):
        return x.reshape(1, -1)

    def wide(w):
        return w.reshape(3, 3 * C1, C1)

    def tall(w):
        return jnp.swapaxes(w, 2, 3).reshape(9 * OC, C3)

    any_spec = pl.BlockSpec(memory_space=pl.ANY)
    vmem_spec = pl.BlockSpec(memory_space=pltpu.VMEM)
    operands = [
        (latent1, any_spec), (flat(norm1a_g), vmem_spec), (flat(norm1a_b), vmem_spec), (wide(conv1a_w), any_spec),
        (flat(norm1b_g), vmem_spec), (flat(norm1b_b), vmem_spec), (wide(conv1b_w), any_spec), (flat(conv1b_b), vmem_spec),
        (feat3, any_spec), (adapter3, any_spec), (flat(norm3a_g), vmem_spec), (flat(norm3a_b), vmem_spec),
        (tall(conv3a_w), any_spec), (flat(norm3b_g), vmem_spec), (flat(norm3b_b), vmem_spec),
        (tall(conv3b_w), any_spec), (flat(conv3b_b), vmem_spec),
    ]
    out1, out3 = pl.pallas_call(
        kernel,
        out_shape=(
            jax.ShapeDtypeStruct((H1, W1, C1), BF16),
            jax.ShapeDtypeStruct((H3, OC, W3), BF16),
        ),
        in_specs=[spec for _, spec in operands],
        out_specs=(any_spec, any_spec),
        scratch_shapes=[
            pltpu.VMEM((H1, W1, C1), BF16),
            pltpu.VMEM((2, W1, C1), BF16),
            pltpu.VMEM((2, W1, C1), BF16),
            pltpu.VMEM((2, 2, 24, C1), F32),
            pltpu.VMEM((2, 2, 24, C1), F32),
            pltpu.VMEM((H1 + 4, WP, 3 * C1), BF16),
            pltpu.VMEM((H1 + 2, WP, C1), F32),
            pltpu.VMEM((3, 3 * C1, C1), BF16),
            pltpu.VMEM((3, 3 * C1, C1), BF16),
            pltpu.VMEM((9 * OC, C3), BF16),
            pltpu.VMEM((9 * OC, C3), BF16),
            pltpu.VMEM((H3, 16, C3), BF16),
            pltpu.VMEM((H3, 16, C3), BF16),
            pltpu.VMEM((C, H3, 16, C3), BF16),
            pltpu.VMEM((C, H3, 16, C3), BF16),
            pltpu.VMEM((C, H3, OC, W3), BF16),
            pltpu.VMEM((H3, 9 * OC, W3), F32),
            pltpu.VMEM((2, 2, OC, W3), F32),
            pltpu.VMEM((2, 2, OC, W3), F32),
            pltpu.VMEM((H3, OC, W3), F32),
            pltpu.VMEM((H3, OC, W3), F32),
            pltpu.VMEM((H1, W1, C1), BF16),
            pltpu.VMEM((H3, OC, W3), BF16),
            pltpu.VMEM((16, 8, 128), F32),
            pltpu.VMEM((16, 8, 128), F32),
            pltpu.VMEM((16, 8, 128), F32),
            pltpu.VMEM((16, 8, 128), F32),
            pltpu.VMEM((16, 8, 128), F32),
            pltpu.SemaphoreType.DMA((9,)),
            pltpu.SemaphoreType.DMA((5,)),
            pltpu.SemaphoreType.DMA((5,)),
            pltpu.SemaphoreType.DMA((2, 2, 4, 2)),
            pltpu.SemaphoreType.DMA((2, 2, 4, 2)),
            pltpu.SemaphoreType.DMA((2, 2, 5, 2)),
            pltpu.SemaphoreType.DMA((2, 2, 5, 2)),
            pltpu.SemaphoreType.DMA((1,)),
            pltpu.SemaphoreType.DMA((4,)),
            pltpu.SemaphoreType.DMA((4,)),
            pltpu.SemaphoreType.DMA((2, 2)),
            pltpu.SemaphoreType.DMA((2, 2)),
        ],
        compiler_params=pltpu.CompilerParams(
            collective_id=0, has_side_effects=True, vmem_limit_bytes=56 * 1024 * 1024
        ),
    )(*[value for value, _ in operands])
    return out1, jnp.swapaxes(out3, 1, 2)


def solution(mesh):
    return jax.shard_map(
        body,
        mesh=mesh,
        in_specs=(
            P("rows", "cols", None), P(), P(), P(), P(), P(), P(), P(),
            P("rows", "cols", None), P("rows", "cols", None), P(), P(),
            P(None, None, None, "cols"), P("cols"), P("cols"), P(None, None, None, "cols"), P("cols"),
        ),
        out_specs=(P("rows", "cols", None), P("rows", None, "cols")),
        check_vma=False,
    )
```

profile of v0, /device:TPU:1, one launch (start us, length us, event | category | flops | bytes accessed | tf_op | source)
XLA Modules:
  0.0 91.8 jit_solution(15411310035784721011)
XLA Ops:
  0.6 1.2 %reshape.46.g1a = f32[1,320]{1,0:T(1,128)} reshape(f32[320]{0:T(512)} %param.18) | data formatting | bytes 2560 | tf_op jit(solution)/shard_map/reshape | solution.py:527
  1.9 1.3 %reshape.47.b1a = f32[1,320]{1,0:T(1,128)} reshape(f32[320]{0:T(512)} %param.19) | data formatting | bytes 2560 | tf_op jit(solution)/shard_map/reshape | solution.py:527
  3.1 1.3 %reshape.49.g1b = f32[1,320]{1,0:T(1,128)} reshape(f32[320]{0:T(512)} %param.21) | data formatting | bytes 2560 | tf_op jit(solution)/shard_map/reshape | solution.py:527
  4.4 1.3 %reshape.50.b1b = f32[1,320]{1,0:T(1,128)} reshape(f32[320]{0:T(512)} %param.22) | data formatting | bytes 2560 | tf_op jit(solution)/shard_map/reshape | solution.py:527
  5.7 1.3 %reshape.52.c1b = f32[1,320]{1,0:T(1,128)} reshape(f32[320]{0:T(512)} %param.24) | data formatting | bytes 2560 | tf_op jit(solution)/shard_map/reshape | solution.py:527
  6.9 1.3 %reshape.53.g3a = f32[1,1280]{1,0:T(1,128)} reshape(f32[1280]{0:T(1024)} %param.27) | data formatting | bytes 10240 | tf_op jit(solution)/shard_map/reshape | solution.py:527
  8.2 1.3 %reshape.54.b3a = f32[1,1280]{1,0:T(1,128)} reshape(f32[1280]{0:T(1024)} %param.28) | data formatting | bytes 10240 | tf_op jit(solution)/shard_map/reshape | solution.py:527
  9.5 78.5 %shard_map.176 = (bf16[16,64,320]{2,1,0:T(8,128)(2,1)}, bf16[4,80,256]{2,1,0:T(8,128)(2,1)}) custom-call(bf16[16,64,320]{2,1,0:T(8,128)(2,1)} %lat_h.1, f32[1,320]{1,0:T(1,128)} %reshape.46.g1a, f32[1,320]{1,0:T(1,128)} %reshape.47.b1a, bf16[3,960,320]{2,1,0:T(8,128)(2,1)} %bitcast.12, f32[1,320]{1,0:T(1,128)} %reshape.49.g1b, f32[1,320]{1,0:T(1,128)} %reshape.50.b1b, ...), custom_call_target="tpu_custom_call" | custom-call | tf_op jit(solution)/shard_map/pallas_call | solution.py:544
  88.1 2.1 %copy.21 = bf16[16,64,320]{2,1,0:T(8,128)(2,1)} copy(bf16[16,64,320]{2,1,0:T(8,128)(2,1)} %get-tuple-element.8) | data formatting | bytes 1310720
  90.2 1.6 %copy.22 = bf16[4,256,80]{1,2,0:T(8,128)(2,1)} copy(bf16[4,256,80]{1,2,0:T(8,128)(2,1)} %bitcast.16) | data formatting | bytes 327680
where the time goes:
time: 92.1 us; the launch traced here: 91.8 us
  Pallas kernels  78.5 us (85%)
  local copies, waits for them, and re-layouts  12.6 us (14%)
    pallas_call x1, Pallas kernels, body(): pl.pallas_call(kernel, out_shape=(jax.ShapeDtypeStruct((H1, W1, C1), BF16...  78.5 us
    reshape x7, local copies, waits for them, and re-layouts, flat(): return x.reshape(1, -1)  8.89 us
    unnamed x2, local copies, waits for them, and re-layouts  3.68 us

commit v1 on v0

--- a/solution.py
+++ b/solution.py
@@ -26,14 +26,31 @@
     return lax.broadcasted_iota(jnp.int32, shape, dim)
 
 
-def group_matrix(chans, width, offset):
-    chan = iota((chans, 128), 0)
-    first = (iota((chans, 128), 1) - offset) * width
-    return jnp.where((chan >= first) & (chan < first + width), 1.0, 0.0).astype(F32)
-
-
-def exact_dot(a, b, dims=(((1,), (0,)), ((), ()))):
-    return lax.dot_general(a, b, dims, precision=lax.Precision.HIGHEST, preferred_element_type=F32)
+def group_matrix(chans, width, offset, dim):
+    shape = (chans, 128) if dim == 0 else (128, chans)
+    chan = iota(shape, dim)
+    first = (iota(shape, 1 - dim) - offset) * width
+    return jnp.where((chan >= first) & (chan < first + width), 1.0, 0.0).astype(BF16)
+
+
+def exact_dot(a, ones):
+    high = a.astype(BF16)
+    rest = a - high.astype(F32)
+    middle = rest.astype(BF16)
+    low = (rest - middle.astype(F32)).astype(BF16)
+    n = a.shape[0]
+    out = jnp.dot(jnp.concatenate([high, middle, low], axis=0), ones, preferred_element_type=F32)
+    return out[0:n] + out[n : 2 * n] + out[2 * n :]
+
+
+def group_sums(sums, squares, ones, offset):
+    both = exact_dot(jnp.concatenate([sums, squares], axis=0), ones)
+    first = pltpu.roll(both[0:8], offset, 1) if offset else both[0:8]
+    return first + pltpu.roll(both[8:16], offset + 32, 1)
+
+
+def flat(ref):
+    return ref[...].reshape(1, -1)
 
 
 def halves(value):
@@ -41,8 +58,10 @@
 
 
 def kernel(
-    lat_h, g1a, b1a, w1a_h, g1b, b1b, w1b_h, c1b, feat_h, adap_h, g3a, b3a, w3a_h, g3b, b3b, w3b_h, c3b,
+    lat_h, g1a_h, b1a_h, w1a_h, g1b_h, b1b_h, w1b_h, c1b_h,
+    feat_h, adap_h, g3a_h, b3a_h, w3a_h, g3b_h, b3b_h, w3b_h, c3b_h,
     out1_h, out3_h,
+    g1a, b1a, g1b, b1b, c1b, g3a, b3a, g3b, b3b, c3b,
     lat, top, bottom, pack, side, act, hid, w1a, w1b, w3a, w3b, feat, adap, gat1, act3, gat2, prod,
     edge_s, edge_r, hid3, res, o1, o3, st_a1, st_a2, st_b1, st_b2, st_c,
     local_sem, ar_send, ar_recv, ring_send, ring_recv, mate_send, mate_recv, own_send,
@@ -70,8 +89,17 @@
         "w1b": local(w1b_h, w1b, 5),
         "w3b": local(w3b_h, w3b, 6),
     }
-    for copy in loads.values():
-        copy.start()
+    small = [
+        local(src, dst, 9 + i)
+        for i, (src, dst) in enumerate(
+            (
+                (g1a_h, g1a), (b1a_h, b1a), (g1b_h, g1b), (b1b_h, b1b), (c1b_h, c1b),
+                (g3a_h, g3a), (b3a_h, b3a), (g3b_h, g3b), (b3b_h, b3b), (c3b_h, c3b),
+            )
+        )
+    ]
+    for name in ("feat", "adap", "lat"):
+        loads[name].start()
 
     barrier = pltpu.get_barrier_semaphore()
     for step in range(1, R):
@@ -178,8 +206,10 @@
         for half in range(2):
             go(mate_copy(which, gat, 0, 0, half))
 
-    def ring_step(which, gat, hop):
+    def ring_step(which, gat, hop, only=None):
         for direction, half in arrivals(hop):
+            if only is not None and half != only:
+                continue
             ring_wait(which, gat, direction, hop, half)
             if (direction, half) in (arrivals(hop + 1) if hop < 4 else []):
                 go(ring_copy(which, gat, direction, hop + 1, half))
@@ -195,6 +225,10 @@
 
     loads["feat"].wait()
     loads["adap"].wait()
+    for copy in small:
+        copy.start()
+    for name in ("w1a", "w3a", "w1b", "w3b"):
+        loads[name].start()
     js = jnp.zeros((8, C3), F32)
     jq = jnp.zeros((8, C3), F32)
     for i in range(H3):
@@ -206,6 +240,7 @@
 
     pl.semaphore_wait(barrier, R - 1 + C - 1)
     ring_start(0, gat1)
+    joined_sums = group_sums(js, jq, group_matrix(C3, 40, 0, 0), 64)
 
     loads["lat"].wait()
 
@@ -230,12 +265,8 @@
         value = lat[i].astype(F32).reshape(8, 8, C1)
         ls = ls + jnp.sum(value, axis=0)
         lq = lq + jnp.sum(value * value, axis=0)
-    st_a1[0] = (
-        exact_dot(ls, group_matrix(C1, 10, 0))
-        + exact_dot(lq, group_matrix(C1, 10, 32))
-        + exact_dot(js, group_matrix(C3, 40, 64))
-        + exact_dot(jq, group_matrix(C3, 40, 96))
-    )
+    ones1 = group_matrix(C1, 10, 0, 0)
+    st_a1[0] = group_sums(ls, lq, ones1, 0) + joined_sums
     spread(st_a1, "rows", 0)
 
     to_down.wait()
@@ -265,9 +296,10 @@
     to_right.start()
     to_left.start()
 
+    ring_step(0, gat1, 1, 0)
     st_a2[0] = collect(st_a1, "rows", 0)
     spread(st_a2, "cols", 1)
-    ring_step(0, gat1, 1)
+    ring_step(0, gat1, 1, 1)
 
     def group_rates(total):
         total = jnp.sum(total, axis=0, keepdims=True)
@@ -282,13 +314,15 @@
         return jnp.where(live, mean, 0.0), jnp.where(live, inverse, 0.0)
 
     def channel_rates(rates, matrix, gain, shift):
-        mean, inverse = (exact_dot(x, matrix, NT)[0:1] for x in rates)
+        both = exact_dot(jnp.where(iota((8, 128), 0) == 0, *rates), matrix)
+        mean, inverse = both[0:1], both[1:2]
         scale = inverse * gain
         return 0.5 * scale, 0.5 * (shift - mean * scale)
 
+    for copy in small:
+        copy.wait()
     rates = group_rates(collect(st_a2, "cols", 1))
-    scale1, shift1 = channel_rates(rates, group_matrix(C1, 10, 0), g1a[...], b1a[...])
-    scale3, shift3 = channel_rates(rates, group_matrix(C3, 40, 64), g3a[...], b3a[...])
+    scale1, shift1 = channel_rates(rates, group_matrix(C1, 10, 0, 1), flat(g1a), flat(b1a))
 
     def put_row(i, value, live):
         value = jnp.where(live, halves(value), 0.0)
@@ -318,9 +352,9 @@
                 live = live & (row < R - 1)
             put_row(i, value * scale1 + shift1, live)
 
-    act1_rows(0, 10)
-    ring_step(0, gat1, 2)
-    act1_rows(10, 20)
+    ring_step(0, gat1, 2, 0)
+    act1_rows(0, 20)
+    ring_step(0, gat1, 2, 1)
 
     def conv1(weights, first, count, width):
         total = None
@@ -343,12 +377,14 @@
 
     loads["w1a"].wait()
     hid[pl.ds(0, 6)] = conv1(w1a, 0, 6, WP)
-    ring_step(0, gat1, 3)
+    scale3, shift3 = channel_rates(rates, group_matrix(C3, 40, 64, 1), flat(g3a), flat(b3a))
+    ring_step(0, gat1, 3, 0)
     hid[pl.ds(6, 6)] = conv1(w1a, 6, 6, WP)
     norm3_hop(0)
+    ring_step(0, gat1, 3, 1)
+    hid[pl.ds(12, 6)] = conv1(w1a, 12, 6, WP)
     norm3_hop(1)
     ring_step(0, gat1, 4)
-    hid[pl.ds(12, 6)] = conv1(w1a, 12, 6, WP)
 
     hs = jnp.zeros((8, C1), F32)
     hq = jnp.zeros((8, C1), F32)
@@ -356,7 +392,7 @@
         value = hid[i + 1, 0:W1, :].reshape(8, 8, C1)
         hs = hs + jnp.sum(value, axis=0)
         hq = hq + jnp.sum(value * value, axis=0)
-    st_b1[0] = exact_dot(hs, group_matrix(C1, 10, 0)) + exact_dot(hq, group_matrix(C1, 10, 32))
+    st_b1[0] = group_sums(hs, hq, ones1, 0)
     spread(st_b1, "rows", 2)
 
     norm3_hop(2)
@@ -441,7 +477,7 @@
     spread(st_c, "rows", 4)
 
     rates = group_rates(collect(st_b2, "cols", 3))
-    scale2, shift2 = channel_rates(rates, group_matrix(C1, 10, 0), g1b[...], b1b[...])
+    scale2, shift2 = channel_rates(rates, group_matrix(C1, 10, 0, 1), flat(g1b), flat(b1b))
     near_ok = (place < W1) | ((place == W1) & (col < C - 1)) | ((place == WP - 1) & (col > 0))
 
     def act2_rows(first, last):
@@ -463,7 +499,7 @@
 
     def upright(ref):
         eye = iota((OC, OC), 0) == iota((OC, OC), 1)
-        return jnp.sum(jnp.where(eye, jnp.broadcast_to(ref[...], (OC, OC)), 0.0), axis=1, keepdims=True)
+        return jnp.sum(jnp.where(eye, jnp.broadcast_to(flat(ref), (OC, OC)), 0.0), axis=1, keepdims=True)
 
     scale4 = inverse * upright(g3b)
     shift4 = 0.5 * (upright(b3b) - mean * scale4)
@@ -476,16 +512,21 @@
     loads["w1b"].wait()
 
     def out1_rows(first, count):
-        value = conv1(w1b, first, count, W1) + c1b[...].reshape(1, 1, C1)
+        value = conv1(w1b, first, count, W1) + flat(c1b).reshape(1, 1, C1)
         o1[pl.ds(first, count)] = (lat[pl.ds(first, count)].astype(F32) + value).astype(BF16)
 
-    ring_step(1, gat2, 1)
-    out1_rows(0, 8)
-    ring_step(1, gat2, 2)
-    out1_rows(8, 8)
+    ring_step(1, gat2, 1, 0)
+    out1_rows(0, 4)
+    ring_step(1, gat2, 1, 1)
+    out1_rows(4, 4)
+    ring_step(1, gat2, 2, 0)
+    out1_rows(8, 4)
+    ring_step(1, gat2, 2, 1)
+    out1_rows(12, 4)
     write1 = local(o1, out1_h, 7)
     write1.start()
-    ring_step(1, gat2, 3)
+    ring_step(1, gat2, 3, 0)
+    ring_step(1, gat2, 3, 1)
 
     pick = jnp.where(iota((OC, C3), 1) == iota((OC, C3), 0) + col * OC, 1.0, 0.0).astype(BF16)
 
@@ -523,9 +564,6 @@
     latent1, norm1a_g, norm1a_b, conv1a_w, norm1b_g, norm1b_b, conv1b_w, conv1b_b,
     feat3, adapter3, norm3a_g, norm3a_b, conv3a_w, norm3b_g, norm3b_b, conv3b_w, conv3b_b,
 ):
-    def flat(x):
-        return x.reshape(1, -1)
-
     def wide(w):
         return w.reshape(3, 3 * C1, C1)
 
@@ -533,13 +571,12 @@
         return jnp.swapaxes(w, 2, 3).reshape(9 * OC, C3)
 
     any_spec = pl.BlockSpec(memory_space=pl.ANY)
-    vmem_spec = pl.BlockSpec(memory_space=pltpu.VMEM)
     operands = [
-        (latent1, any_spec), (flat(norm1a_g), vmem_spec), (flat(norm1a_b), vmem_spec), (wide(conv1a_w), any_spec),
-        (flat(norm1b_g), vmem_spec), (flat(norm1b_b), vmem_spec), (wide(conv1b_w), any_spec), (flat(conv1b_b), vmem_spec),
-        (feat3, any_spec), (adapter3, any_spec), (flat(norm3a_g), vmem_spec), (flat(norm3a_b), vmem_spec),
-        (tall(conv3a_w), any_spec), (flat(norm3b_g), vmem_spec), (flat(norm3b_b), vmem_spec),
-        (tall(conv3b_w), any_spec), (flat(conv3b_b), vmem_spec),
+        (latent1, any_spec), (norm1a_g, any_spec), (norm1a_b, any_spec), (wide(conv1a_w), any_spec),
+        (norm1b_g, any_spec), (norm1b_b, any_spec), (wide(conv1b_w), any_spec), (conv1b_b, any_spec),
+        (feat3, any_spec), (adapter3, any_spec), (norm3a_g, any_spec), (norm3a_b, any_spec),
+        (tall(conv3a_w), any_spec), (norm3b_g, any_spec), (norm3b_b, any_spec),
+        (tall(conv3b_w), any_spec), (conv3b_b, any_spec),
     ]
     out1, out3 = pl.pallas_call(
         kernel,
@@ -550,6 +587,7 @@
         in_specs=[spec for _, spec in operands],
         out_specs=(any_spec, any_spec),
         scratch_shapes=[
+            *[pltpu.VMEM((n,), F32) for n in (C1, C1, C1, C1, C1, C3, C3, OC, OC, OC)],
             pltpu.VMEM((H1, W1, C1), BF16),
             pltpu.VMEM((2, W1, C1), BF16),
             pltpu.VMEM((2, W1, C1), BF16),
@@ -578,7 +616,7 @@
             pltpu.VMEM((16, 8, 128), F32),
             pltpu.VMEM((16, 8, 128), F32),
             pltpu.VMEM((16, 8, 128), F32),
-            pltpu.SemaphoreType.DMA((9,)),
+            pltpu.SemaphoreType.DMA((19,)),
             pltpu.SemaphoreType.DMA((5,)),
             pltpu.SemaphoreType.DMA((5,)),
             pltpu.SemaphoreType.DMA((2, 2, 4, 2)),

time: 92.1 us -> 81.5 us (0.88)
  local copies, waits for them, and re-layouts: 12.6 us -> 3.68 us
  Pallas kernels: 78.5 us -> 77 us
    reshape x7 -> x0, local copies, waits for them, and re-layouts: 8.89 us -> none  [flat(): return x.reshape(1, -1)]
    pallas_call x1, Pallas kernels: 78.5 us -> 77 us  [body(): pl.pallas_call(kernel, out_shape=(jax.ShapeDtypeStruct((H1, W1, C1), BF16...]
where the time goes in v1:
time: 81.5 us; the launch traced here: 81.4 us
  Pallas kernels  77 us (94%)
  local copies, waits for them, and re-layouts  3.68 us (5%)
    pallas_call x1, Pallas kernels, body(): pl.pallas_call(kernel, out_shape=(jax.ShapeDtypeStruct((H1, W1, C1), BF16...  77 us
    unnamed x2, local copies, waits for them, and re-layouts  3.68 us

profile of v1, /device:TPU:1, one launch (start us, length us, event | category | flops | bytes accessed | tf_op | source)
XLA Modules:
  0.0 81.4 jit_solution(2616117618887392341)
XLA Ops:
  0.6 77.0 %shard_map.176 = (bf16[16,64,320]{2,1,0:T(8,128)(2,1)}, bf16[4,80,256]{2,1,0:T(8,128)(2,1)}) custom-call(bf16[16,64,320]{2,1,0:T(8,128)(2,1)} %lat_h.1, f32[320]{0:T(512)} %g1a_h.1, f32[320]{0:T(512)} %b1a_h.1, bf16[3,960,320]{2,1,0:T(8,128)(2,1)} %bitcast.9, f32[320]{0:T(512)} %g1b_h.1, f32[320]{0:T(512)} %b1b_h.1, bf16[3,960,320]{2,1,0:T(8,128)(2,1)} %bitcast.10, ...), custom_call_target="tpu_custom_call" | custom-call | tf_op jit(solution)/shard_map/pallas_call | solution.py:581
  77.7 2.1 %copy.21 = bf16[16,64,320]{2,1,0:T(8,128)(2,1)} copy(bf16[16,64,320]{2,1,0:T(8,128)(2,1)} %get-tuple-element.8) | data formatting | bytes 1310720
  79.8 1.6 %copy.22 = bf16[4,256,80]{1,2,0:T(8,128)(2,1)} copy(bf16[4,256,80]{1,2,0:T(8,128)(2,1)} %bitcast.13) | data formatting | bytes 327680

commit v2 on v1

--- a/solution.py
+++ b/solution.py
@@ -17,6 +17,7 @@
 H1, W1 = 16, 64
 H3, W3 = 4, 256
 WP = 80
+ORDER = (1, 2, 0, 3)
 NT = (((1,), (1,)), ((), ()))
 COUNT1 = float(R * H1 * C * W1 * (C1 // 32))
 COUNT3 = float(R * H3 * W3 * (C3 // 32))
@@ -63,8 +64,8 @@
     out1_h, out3_h,
     g1a, b1a, g1b, b1b, c1b, g3a, b3a, g3b, b3b, c3b,
     lat, top, bottom, pack, side, act, hid, w1a, w1b, w3a, w3b, feat, adap, gat1, act3, gat2, prod,
-    edge_s, edge_r, hid3, res, o1, o3, st_a1, st_a2, st_b1, st_b2, st_c,
-    local_sem, ar_send, ar_recv, ring_send, ring_recv, mate_send, mate_recv, own_send,
+    edge_s, edge_r, hid3, res, o1, o3, st_a1, st_a2, st_b1, st_b2, st_c, st_d, act4,
+    local_sem, ar_send, ar_recv, ring_send, ring_recv, mate_send, mate_recv,
     halo_send, halo_recv, edge_send, edge_recv,
 ):
     row = lax.axis_index("rows")
@@ -123,7 +124,7 @@
 
         lax.fori_loop(1, 16, send, 0)
 
-    def collect(buf, axis, index):
+    def arrived(buf, axis, index):
         rest = pltpu.make_async_remote_copy(
             src_ref=buf.at[pl.ds(1, 15)],
             dst_ref=buf.at[pl.ds(1, 15)],
@@ -134,13 +135,16 @@
         )
         rest.wait_recv()
         rest.wait_send()
+
+    def collect(buf, axis, index):
+        arrived(buf, axis, index)
         return jnp.sum(buf[...], axis=0)
 
     def origin(direction, hop):
         return (z + Z - hop) % Z if direction == 0 else (z + hop) % Z
 
     def chunk(gat, slot, half):
-        return gat.at[slot, pl.ds(2 * half, 2)]
+        return gat.at[slot, half]
 
     def ring_copy(which, gat, direction, hop, half):
         slot = 2 * origin(direction, hop - 1) + core
@@ -188,10 +192,13 @@
             device_id_type=MESH,
         ).wait_recv()
 
-    def arrivals(hop):
+    def arrivals(hop, k):
         if hop == 4:
-            return [(0, 0), (1, 1)]
-        return [(direction, half) for half in range(2) for direction in range(2)]
+            return [(0, 1 - k), (1, 2 + k)]
+        return [(0, ORDER[k]), (1, ORDER[k])]
+
+    def steps(hop):
+        return range(2 if hop == 4 else H3)
 
     sends = []
 
@@ -199,29 +206,30 @@
         copy.start()
         sends.append(copy)
 
-    def ring_start(which, gat):
-        for half in range(2):
+    def ring_start(which, gat, parts):
+        for part in parts:
             for direction in range(2):
-                go(ring_copy(which, gat, direction, 1, half))
-        for half in range(2):
-            go(mate_copy(which, gat, 0, 0, half))
-
-    def ring_step(which, gat, hop, only=None):
-        for direction, half in arrivals(hop):
-            if only is not None and half != only:
-                continue
-            ring_wait(which, gat, direction, hop, half)
-            if (direction, half) in (arrivals(hop + 1) if hop < 4 else []):
-                go(ring_copy(which, gat, direction, hop + 1, half))
-            go(mate_copy(which, gat, direction, hop, half))
+                go(ring_copy(which, gat, direction, 1, part))
+        for part in parts:
+            go(mate_copy(which, gat, 0, 0, part))
+
+    def ring_step(which, gat, hop, *ks):
+        last = [pair for k in range(2) for pair in arrivals(4, k)]
+        for k in ks:
+            for direction, part in arrivals(hop, k):
+                ring_wait(which, gat, direction, hop, part)
+                if hop < 3 or (hop == 3 and (direction, part) in last):
+                    go(ring_copy(which, gat, direction, hop + 1, part))
+                go(mate_copy(which, gat, direction, hop, part))
 
     def mate_step(which, gat, hop):
         if hop == 0:
-            for half in range(2):
-                mate_wait(which, gat, 0, 0, half)
+            for part in range(H3):
+                mate_wait(which, gat, 0, 0, part)
         else:
-            for direction, half in arrivals(hop):
-                mate_wait(which, gat, direction, hop, half)
+            for k in steps(hop):
+                for direction, part in arrivals(hop, k):
+                    mate_wait(which, gat, direction, hop, part)
 
     loads["feat"].wait()
     loads["adap"].wait()
@@ -239,7 +247,7 @@
         jq = jq + jnp.sum(value * value, axis=0)
 
     pl.semaphore_wait(barrier, R - 1 + C - 1)
-    ring_start(0, gat1)
+    ring_start(0, gat1, ORDER)
     joined_sums = group_sums(js, jq, group_matrix(C3, 40, 0, 0), 64)
 
     loads["lat"].wait()
@@ -296,10 +304,10 @@
     to_right.start()
     to_left.start()
 
-    ring_step(0, gat1, 1, 0)
+    ring_step(0, gat1, 1, 0, 1)
     st_a2[0] = collect(st_a1, "rows", 0)
     spread(st_a2, "cols", 1)
-    ring_step(0, gat1, 1, 1)
+    ring_step(0, gat1, 1, 2, 3)
 
     def group_rates(total):
         total = jnp.sum(total, axis=0, keepdims=True)
@@ -352,9 +360,9 @@
                 live = live & (row < R - 1)
             put_row(i, value * scale1 + shift1, live)
 
-    ring_step(0, gat1, 2, 0)
+    ring_step(0, gat1, 2, 0, 1)
     act1_rows(0, 20)
-    ring_step(0, gat1, 2, 1)
+    ring_step(0, gat1, 2, 2, 3)
 
     def conv1(weights, first, count, width):
         total = None
@@ -378,13 +386,13 @@
     loads["w1a"].wait()
     hid[pl.ds(0, 6)] = conv1(w1a, 0, 6, WP)
     scale3, shift3 = channel_rates(rates, group_matrix(C3, 40, 64, 1), flat(g3a), flat(b3a))
-    ring_step(0, gat1, 3, 0)
+    ring_step(0, gat1, 3, 0, 1)
     hid[pl.ds(6, 6)] = conv1(w1a, 6, 6, WP)
     norm3_hop(0)
-    ring_step(0, gat1, 3, 1)
+    ring_step(0, gat1, 3, 2, 3)
     hid[pl.ds(12, 6)] = conv1(w1a, 12, 6, WP)
     norm3_hop(1)
-    ring_step(0, gat1, 4)
+    ring_step(0, gat1, 4, 0, 1)
 
     hs = jnp.zeros((8, C1), F32)
     hq = jnp.zeros((8, C1), F32)
@@ -399,12 +407,9 @@
     norm3_hop(3)
     norm3_hop(4)
 
-    def taps(weights, source, dims):
-        def one(i, carry):
+    def taps(weights, source, dims, rows_of):
+        for i in rows_of:
             prod[i] = lax.dot_general(weights[...], source(i), dims, preferred_element_type=F32)
-            return carry
-
-        lax.fori_loop(0, H3, one, 0)
 
     lane3 = iota((OC, W3), 1)
 
@@ -449,17 +454,25 @@
         return low, high
 
     loads["w3a"].wait()
-    taps(w3a, lambda i: act3[:, i].reshape(W3, C3), NT)
+    taps(w3a, lambda i: act3[:, i].reshape(W3, C3), NT, (0, 3))
     copies = edges_out(0)
+    taps(w3a, lambda i: act3[:, i].reshape(W3, C3), NT, (1, 2))
+    for i in (1, 2):
+        value = combine(i)
+        hid3[i] = value
+        gat2[col, i] = value.astype(BF16)
+    ring_start(1, gat2, (1, 2))
     st_b2[0] = collect(st_b1, "rows", 2)
     spread(st_b2, "cols", 3)
-    for i in range(H3):
+    for i in (0, 3):
         hid3[i] = combine(i)
     for copy in copies:
         copy.wait()
-    low, high = edges_in(0)
-    hid3[0] = hid3[0] + low
-    hid3[H3 - 1] = hid3[H3 - 1] + high
+    for i, border in zip((0, 3), edges_in(0)):
+        value = hid3[i] + border
+        hid3[i] = value
+        gat2[col, i] = value.astype(BF16)
+    ring_start(1, gat2, (0, 3))
 
     fs = jnp.zeros((OC, W3), F32)
     fq = jnp.zeros((OC, W3), F32)
@@ -489,7 +502,8 @@
                 live = live & (row < R - 1)
             put_row(i, hid[i] * scale2 + shift2, live)
 
-    act2_rows(0, 6)
+    ring_step(1, gat2, 1, 0, 1)
+    act2_rows(0, 9)
 
     total = jnp.sum(collect(st_c, "rows", 4), axis=0, keepdims=True)
     total = jnp.broadcast_to(total, (OC, 128)) / COUNT3
@@ -504,29 +518,44 @@
     scale4 = inverse * upright(g3b)
     shift4 = 0.5 * (upright(b3b) - mean * scale4)
     scale4 = 0.5 * scale4
-    for i in range(H3):
-        gat2[col, i] = halves(hid3[i] * scale4 + shift4).astype(BF16)
-    ring_start(1, gat2)
-
-    act2_rows(6, 18)
+    eye = iota((OC, 128), 0) == iota((OC, 128), 1)
+    as_rows = [jnp.sum(jnp.where(eye, x, 0.0), axis=0, keepdims=True) for x in (scale4, shift4)]
+    st_d[0] = jnp.where(iota((8, 128), 0) == 0, *as_rows)
+    spread(st_d, "cols", 5)
+
+    act2_rows(9, 18)
+    ring_step(1, gat2, 1, 2, 3)
     loads["w1b"].wait()
+
+    def norm4(slot):
+        block = st_d[(col + C - slot) % C]
+        scale, shift = (jnp.sum(jnp.where(eye, block[j : j + 1], 0.0), axis=1, keepdims=True) for j in range(2))
+        for i in range(H3):
+            act4[slot, i] = halves(gat2[slot, i].astype(F32) * scale + shift).astype(BF16)
+
+    def norm4_hop(hop):
+        mate_step(1, gat2, hop)
+        for direction in range(1 if hop in (0, 4) else 2):
+            for k in range(2):
+                norm4(2 * origin(direction, hop) + k)
 
     def out1_rows(first, count):
         value = conv1(w1b, first, count, W1) + flat(c1b).reshape(1, 1, C1)
         o1[pl.ds(first, count)] = (lat[pl.ds(first, count)].astype(F32) + value).astype(BF16)
 
-    ring_step(1, gat2, 1, 0)
     out1_rows(0, 4)
-    ring_step(1, gat2, 1, 1)
+    ring_step(1, gat2, 2, 0, 1)
+    arrived(st_d, "cols", 5)
+    norm4_hop(0)
     out1_rows(4, 4)
-    ring_step(1, gat2, 2, 0)
+    ring_step(1, gat2, 2, 2, 3)
     out1_rows(8, 4)
-    ring_step(1, gat2, 2, 1)
+    norm4_hop(1)
+    ring_step(1, gat2, 3, 0, 1)
     out1_rows(12, 4)
     write1 = local(o1, out1_h, 7)
     write1.start()
-    ring_step(1, gat2, 3, 0)
-    ring_step(1, gat2, 3, 1)
+    ring_step(1, gat2, 3, 2, 3)
 
     pick = jnp.where(iota((OC, C3), 1) == iota((OC, C3), 0) + col * OC, 1.0, 0.0).astype(BF16)
 
@@ -536,13 +565,15 @@
 
     lax.fori_loop(0, H3, residual, 0)
     bias3 = upright(c3b)
-    ring_step(1, gat2, 4)
-    for hop in range(5):
-        mate_step(1, gat2, hop)
+    norm4_hop(2)
+    ring_step(1, gat2, 4, 0, 1)
+    norm4_hop(3)
+    norm4_hop(4)
 
     loads["w3b"].wait()
-    taps(w3b, lambda i: gat2[:, i].reshape(C3, W3), (((1,), (0,)), ((), ())))
+    taps(w3b, lambda i: act4[:, i].reshape(C3, W3), (((1,), (0,)), ((), ())), (0, 3))
     copies = edges_out(1)
+    taps(w3b, lambda i: act4[:, i].reshape(C3, W3), (((1,), (0,)), ((), ())), (1, 2))
     for i in range(H3):
         res[i] = res[i] + combine(i) + bias3
     for copy in copies:
@@ -616,14 +647,15 @@
             pltpu.VMEM((16, 8, 128), F32),
             pltpu.VMEM((16, 8, 128), F32),
             pltpu.VMEM((16, 8, 128), F32),
+            pltpu.VMEM((16, 8, 128), F32),
+            pltpu.VMEM((C, H3, OC, W3), BF16),
             pltpu.SemaphoreType.DMA((19,)),
-            pltpu.SemaphoreType.DMA((5,)),
-            pltpu.SemaphoreType.DMA((5,)),
-            pltpu.SemaphoreType.DMA((2, 2, 4, 2)),
-            pltpu.SemaphoreType.DMA((2, 2, 4, 2)),
-            pltpu.SemaphoreType.DMA((2, 2, 5, 2)),
-            pltpu.SemaphoreType.DMA((2, 2, 5, 2)),
-            pltpu.SemaphoreType.DMA((1,)),
+            pltpu.SemaphoreType.DMA((6,)),
+            pltpu.SemaphoreType.DMA((6,)),
+            pltpu.SemaphoreType.DMA((2, 2, 4, 4)),
+            pltpu.SemaphoreType.DMA((2, 2, 4, 4)),
+            pltpu.SemaphoreType.DMA((2, 2, 5, 4)),
+            pltpu.SemaphoreType.DMA((2, 2, 5, 4)),
             pltpu.SemaphoreType.DMA((4,)),
             pltpu.SemaphoreType.DMA((4,)),
             pltpu.SemaphoreType.DMA((2, 2)),

time: 81.5 us -> 77 us (0.945)
  Pallas kernels: 77 us -> 72.5 us
    pallas_call x1, Pallas kernels: 77 us -> 72.5 us  [body(): pl.pallas_call(kernel, out_shape=(jax.ShapeDtypeStruct((H1, W1, C1), BF16...]
where the time goes in v2:
time: 77 us; the launch traced here: 76.8 us
  Pallas kernels  72.5 us (94%)
  local copies, waits for them, and re-layouts  3.68 us (5%)
    pallas_call x1, Pallas kernels, body(): pl.pallas_call(kernel, out_shape=(jax.ShapeDtypeStruct((H1, W1, C1), BF16...  72.5 us
    unnamed x2, local copies, waits for them, and re-layouts  3.68 us

profile of v2, /device:TPU:1, one launch (start us, length us, event | category | flops | bytes accessed | tf_op | source)
XLA Modules:
  0.0 76.8 jit_solution(16954293420821241909)
XLA Ops:
  0.6 72.5 %shard_map.176 = (bf16[16,64,320]{2,1,0:T(8,128)(2,1)}, bf16[4,80,256]{2,1,0:T(8,128)(2,1)}) custom-call(bf16[16,64,320]{2,1,0:T(8,128)(2,1)} %lat_h.1, f32[320]{0:T(512)} %g1a_h.1, f32[320]{0:T(512)} %b1a_h.1, bf16[3,960,320]{2,1,0:T(8,128)(2,1)} %bitcast.9, f32[320]{0:T(512)} %g1b_h.1, f32[320]{0:T(512)} %b1b_h.1, bf16[3,960,320]{2,1,0:T(8,128)(2,1)} %bitcast.10, ...), custom_call_target="tpu_custom_call" | custom-call | tf_op jit(solution)/shard_map/pallas_call | solution.py:612
  73.1 2.1 %copy.21 = bf16[16,64,320]{2,1,0:T(8,128)(2,1)} copy(bf16[16,64,320]{2,1,0:T(8,128)(2,1)} %get-tuple-element.8) | data formatting | bytes 1310720
  75.2 1.6 %copy.22 = bf16[4,256,80]{1,2,0:T(8,128)(2,1)} copy(bf16[4,256,80]{1,2,0:T(8,128)(2,1)} %bitcast.13) | data formatting | bytes 327680

commit v3 on v2

--- a/solution.py
+++ b/solution.py
@@ -170,27 +170,21 @@
             device_id_type=MESH,
         ).wait_recv()
 
-    def mate_copy(which, gat, direction, hop, half):
-        slot = 2 * origin(direction, hop) + core
+    def whole(gat, slot, direction, hop):
+        if hop == 4:
+            return gat.at[slot, pl.ds(2 * direction, 2)]
+        return gat.at[slot]
+
+    def mate_copy(which, gat, direction, hop, side_core):
+        part = whole(gat, 2 * origin(direction, hop) + side_core, direction, hop)
         return pltpu.make_async_remote_copy(
-            src_ref=chunk(gat, slot, half),
-            dst_ref=chunk(gat, slot, half),
-            send_sem=mate_send.at[which, direction, hop, half],
-            recv_sem=mate_recv.at[which, direction, hop, half],
+            src_ref=part,
+            dst_ref=part,
+            send_sem=mate_send.at[which, direction, hop],
+            recv_sem=mate_recv.at[which, direction, hop],
             device_id={"cols": mate},
             device_id_type=MESH,
         )
-
-    def mate_wait(which, gat, direction, hop, half):
-        slot = 2 * origin(direction, hop) + (1 - core)
-        pltpu.make_async_remote_copy(
-            src_ref=chunk(gat, slot, half),
-            dst_ref=chunk(gat, slot, half),
-            send_sem=mate_send.at[which, direction, hop, half],
-            recv_sem=mate_recv.at[which, direction, hop, half],
-            device_id={"cols": mate},
-            device_id_type=MESH,
-        ).wait_recv()
 
     def arrivals(hop, k):
         if hop == 4:
@@ -210,8 +204,8 @@
         for part in parts:
             for direction in range(2):
                 go(ring_copy(which, gat, direction, 1, part))
-        for part in parts:
-            go(mate_copy(which, gat, 0, 0, part))
+        if 3 in parts:
+            go(mate_copy(which, gat, 0, 0, core))
 
     def ring_step(which, gat, hop, *ks):
         last = [pair for k in range(2) for pair in arrivals(4, k)]
@@ -220,16 +214,12 @@
                 ring_wait(which, gat, direction, hop, part)
                 if hop < 3 or (hop == 3 and (direction, part) in last):
                     go(ring_copy(which, gat, direction, hop + 1, part))
-                go(mate_copy(which, gat, direction, hop, part))
+                if k == steps(hop)[-1]:
+                    go(mate_copy(which, gat, direction, hop, core))
 
     def mate_step(which, gat, hop):
-        if hop == 0:
-            for part in range(H3):
-                mate_wait(which, gat, 0, 0, part)
-        else:
-            for k in steps(hop):
-                for direction, part in arrivals(hop, k):
-                    mate_wait(which, gat, direction, hop, part)
+        for direction in range(1 if hop == 0 else 2):
+            mate_copy(which, gat, direction, hop, 1 - core).wait_recv()
 
     loads["feat"].wait()
     loads["adap"].wait()
@@ -276,6 +266,7 @@
     ones1 = group_matrix(C1, 10, 0, 0)
     st_a1[0] = group_sums(ls, lq, ones1, 0) + joined_sums
     spread(st_a1, "rows", 0)
+    ring_step(0, gat1, 1, 0, 1)
 
     to_down.wait()
     to_up.wait()
@@ -304,10 +295,13 @@
     to_right.start()
     to_left.start()
 
-    ring_step(0, gat1, 1, 0, 1)
+    ring_step(0, gat1, 1, 2, 3)
     st_a2[0] = collect(st_a1, "rows", 0)
     spread(st_a2, "cols", 1)
-    ring_step(0, gat1, 1, 2, 3)
+    ring_step(0, gat1, 2, 0, 1, 2, 3)
+    to_right.wait()
+    to_left.wait()
+    ring_step(0, gat1, 3, 0, 1)
 
     def group_rates(total):
         total = jnp.sum(total, axis=0, keepdims=True)
@@ -340,8 +334,6 @@
 
     place = iota((WP, C1), 0)
 
-    to_right.wait()
-    to_left.wait()
     slab_place = iota((16, C1), 0)
     wide_ok = (place < W1) | ((place < W1 + 2) & (col < C - 1)) | ((place >= WP - 2) & (col > 0))
 
@@ -360,9 +352,8 @@
                 live = live & (row < R - 1)
             put_row(i, value * scale1 + shift1, live)
 
-    ring_step(0, gat1, 2, 0, 1)
     act1_rows(0, 20)
-    ring_step(0, gat1, 2, 2, 3)
+    ring_step(0, gat1, 3, 2, 3)
 
     def conv1(weights, first, count, width):
         total = None
@@ -386,13 +377,12 @@
     loads["w1a"].wait()
     hid[pl.ds(0, 6)] = conv1(w1a, 0, 6, WP)
     scale3, shift3 = channel_rates(rates, group_matrix(C3, 40, 64, 1), flat(g3a), flat(b3a))
-    ring_step(0, gat1, 3, 0, 1)
-    hid[pl.ds(6, 6)] = conv1(w1a, 6, 6, WP)
     norm3_hop(0)
-    ring_step(0, gat1, 3, 2, 3)
-    hid[pl.ds(12, 6)] = conv1(w1a, 12, 6, WP)
     norm3_hop(1)
     ring_step(0, gat1, 4, 0, 1)
+    hid[pl.ds(6, 6)] = conv1(w1a, 6, 6, WP)
+    norm3_hop(2)
+    hid[pl.ds(12, 6)] = conv1(w1a, 12, 6, WP)
 
     hs = jnp.zeros((8, C1), F32)
     hq = jnp.zeros((8, C1), F32)
@@ -403,7 +393,6 @@
     st_b1[0] = group_sums(hs, hq, ones1, 0)
     spread(st_b1, "rows", 2)
 
-    norm3_hop(2)
     norm3_hop(3)
     norm3_hop(4)
 
@@ -462,8 +451,6 @@
         hid3[i] = value
         gat2[col, i] = value.astype(BF16)
     ring_start(1, gat2, (1, 2))
-    st_b2[0] = collect(st_b1, "rows", 2)
-    spread(st_b2, "cols", 3)
     for i in (0, 3):
         hid3[i] = combine(i)
     for copy in copies:
@@ -489,6 +476,37 @@
     st_c[0] = jnp.sum(laid.reshape(OC // 8, 8, 128), axis=0)
     spread(st_c, "rows", 4)
 
+    pick = jnp.where(iota((OC, C3), 1) == iota((OC, C3), 0) + col * OC, 1.0, 0.0).astype(BF16)
+
+    def residual(i, carry):
+        res[i] = lax.dot_general(pick, gat1[:, i].reshape(W3, C3), NT, preferred_element_type=F32)
+        return carry
+
+    lax.fori_loop(0, H3, residual, 0)
+    ring_step(1, gat2, 1, 0, 1)
+    st_b2[0] = collect(st_b1, "rows", 2)
+    spread(st_b2, "cols", 3)
+
+    total = jnp.sum(collect(st_c, "rows", 4), axis=0, keepdims=True)
+    total = jnp.broadcast_to(total, (OC, 128)) / COUNT3
+    mean = jnp.sum(jnp.where(lane == group, total, 0.0), axis=1, keepdims=True)
+    square = jnp.sum(jnp.where(lane == group + 2, total, 0.0), axis=1, keepdims=True)
+    inverse = lax.rsqrt(square - mean * mean + EPS)
+
+    def upright(ref):
+        eye = iota((OC, OC), 0) == iota((OC, OC), 1)
+        return jnp.sum(jnp.where(eye, jnp.broadcast_to(flat(ref), (OC, OC)), 0.0), axis=1, keepdims=True)
+
+    scale4 = inverse * upright(g3b)
+    shift4 = 0.5 * (upright(b3b) - mean * scale4)
+    scale4 = 0.5 * scale4
+    eye = iota((OC, 128), 0) == iota((OC, 128), 1)
+    as_rows = [jnp.sum(jnp.where(eye, x, 0.0), axis=0, keepdims=True) for x in (scale4, shift4)]
+    st_d[0] = jnp.where(iota((8, 128), 0) == 0, *as_rows)
+    spread(st_d, "cols", 5)
+
+    ring_step(1, gat2, 1, 2, 3)
+    ring_step(1, gat2, 2, 0, 1, 2)
     rates = group_rates(collect(st_b2, "cols", 3))
     scale2, shift2 = channel_rates(rates, group_matrix(C1, 10, 0, 1), flat(g1b), flat(b1b))
     near_ok = (place < W1) | ((place == W1) & (col < C - 1)) | ((place == WP - 1) & (col > 0))
@@ -502,29 +520,9 @@
                 live = live & (row < R - 1)
             put_row(i, hid[i] * scale2 + shift2, live)
 
-    ring_step(1, gat2, 1, 0, 1)
-    act2_rows(0, 9)
-
-    total = jnp.sum(collect(st_c, "rows", 4), axis=0, keepdims=True)
-    total = jnp.broadcast_to(total, (OC, 128)) / COUNT3
-    mean = jnp.sum(jnp.where(lane == group, total, 0.0), axis=1, keepdims=True)
-    square = jnp.sum(jnp.where(lane == group + 2, total, 0.0), axis=1, keepdims=True)
-    inverse = lax.rsqrt(square - mean * mean + EPS)
-
-    def upright(ref):
-        eye = iota((OC, OC), 0) == iota((OC, OC), 1)
-        return jnp.sum(jnp.where(eye, jnp.broadcast_to(flat(ref), (OC, OC)), 0.0), axis=1, keepdims=True)
-
-    scale4 = inverse * upright(g3b)
-    shift4 = 0.5 * (upright(b3b) - mean * scale4)
-    scale4 = 0.5 * scale4
-    eye = iota((OC, 128), 0) == iota((OC, 128), 1)
-    as_rows = [jnp.sum(jnp.where(eye, x, 0.0), axis=0, keepdims=True) for x in (scale4, shift4)]
-    st_d[0] = jnp.where(iota((8, 128), 0) == 0, *as_rows)
-    spread(st_d, "cols", 5)
-
-    act2_rows(9, 18)
-    ring_step(1, gat2, 1, 2, 3)
+    act2_rows(0, 18)
+    ring_step(1, gat2, 2, 3)
+    ring_step(1, gat2, 3, 0)
     loads["w1b"].wait()
 
     def norm4(slot):
@@ -544,29 +542,20 @@
         o1[pl.ds(first, count)] = (lat[pl.ds(first, count)].astype(F32) + value).astype(BF16)
 
     out1_rows(0, 4)
-    ring_step(1, gat2, 2, 0, 1)
     arrived(st_d, "cols", 5)
     norm4_hop(0)
+    ring_step(1, gat2, 3, 1, 2)
     out1_rows(4, 4)
-    ring_step(1, gat2, 2, 2, 3)
+    norm4_hop(1)
+    ring_step(1, gat2, 3, 3)
     out1_rows(8, 4)
-    norm4_hop(1)
-    ring_step(1, gat2, 3, 0, 1)
+    ring_step(1, gat2, 4, 0)
     out1_rows(12, 4)
     write1 = local(o1, out1_h, 7)
     write1.start()
-    ring_step(1, gat2, 3, 2, 3)
-
-    pick = jnp.where(iota((OC, C3), 1) == iota((OC, C3), 0) + col * OC, 1.0, 0.0).astype(BF16)
-
-    def residual(i, carry):
-        res[i] = lax.dot_general(pick, gat1[:, i].reshape(W3, C3), NT, preferred_element_type=F32)
-        return carry
-
-    lax.fori_loop(0, H3, residual, 0)
+    ring_step(1, gat2, 4, 1)
     bias3 = upright(c3b)
     norm4_hop(2)
-    ring_step(1, gat2, 4, 0, 1)
     norm4_hop(3)
     norm4_hop(4)
 
@@ -654,8 +643,8 @@
             pltpu.SemaphoreType.DMA((6,)),
             pltpu.SemaphoreType.DMA((2, 2, 4, 4)),
             pltpu.SemaphoreType.DMA((2, 2, 4, 4)),
-            pltpu.SemaphoreType.DMA((2, 2, 5, 4)),
-            pltpu.SemaphoreType.DMA((2, 2, 5, 4)),
+            pltpu.SemaphoreType.DMA((2, 2, 5)),
+            pltpu.SemaphoreType.DMA((2, 2, 5)),
             pltpu.SemaphoreType.DMA((4,)),
             pltpu.SemaphoreType.DMA((4,)),
             pltpu.SemaphoreType.DMA((2, 2)),

time: 77 us -> 74.5 us (0.968)
  Pallas kernels: 72.5 us -> 70 us
    pallas_call x1, Pallas kernels: 72.5 us -> 70 us  [body(): pl.pallas_call(kernel, out_shape=(jax.ShapeDtypeStruct((H1, W1, C1), BF16...]
where the time goes in v3:
time: 74.5 us; the launch traced here: 74.4 us
  Pallas kernels  70 us (94%)
  local copies, waits for them, and re-layouts  3.68 us (5%)
    pallas_call x1, Pallas kernels, body(): pl.pallas_call(kernel, out_shape=(jax.ShapeDtypeStruct((H1, W1, C1), BF16...  70 us
    unnamed x2, local copies, waits for them, and re-layouts  3.68 us

profile of v3, /device:TPU:1, one launch (start us, length us, event | category | flops | bytes accessed | tf_op | source)
XLA Modules:
  0.0 74.4 jit_solution(15675247151338428425)
XLA Ops:
  0.6 70.0 %shard_map.176 = (bf16[16,64,320]{2,1,0:T(8,128)(2,1)}, bf16[4,80,256]{2,1,0:T(8,128)(2,1)}) custom-call(bf16[16,64,320]{2,1,0:T(8,128)(2,1)} %lat_h.1, f32[320]{0:T(512)} %g1a_h.1, f32[320]{0:T(512)} %b1a_h.1, bf16[3,960,320]{2,1,0:T(8,128)(2,1)} %bitcast.9, f32[320]{0:T(512)} %g1b_h.1, f32[320]{0:T(512)} %b1b_h.1, bf16[3,960,320]{2,1,0:T(8,128)(2,1)} %bitcast.10, ...), custom_call_target="tpu_custom_call" | custom-call | tf_op jit(solution)/shard_map/pallas_call | solution.py:601
  70.7 2.1 %copy.21 = bf16[16,64,320]{2,1,0:T(8,128)(2,1)} copy(bf16[16,64,320]{2,1,0:T(8,128)(2,1)} %get-tuple-element.8) | data formatting | bytes 1310720
  72.8 1.6 %copy.22 = bf16[4,256,80]{1,2,0:T(8,128)(2,1)} copy(bf16[4,256,80]{1,2,0:T(8,128)(2,1)} %bitcast.13) | data formatting | bytes 327680

commit v4 on v3

--- a/solution.py
+++ b/solution.py
@@ -17,7 +17,7 @@
 H1, W1 = 16, 64
 H3, W3 = 4, 256
 WP = 80
-ORDER = (1, 2, 0, 3)
+ORDERS = ((0, 3, 1, 2), (1, 2, 0, 3))
 NT = (((1,), (1,)), ((), ()))
 COUNT1 = float(R * H1 * C * W1 * (C1 // 32))
 COUNT3 = float(R * H3 * W3 * (C3 // 32))
@@ -170,13 +170,10 @@
             device_id_type=MESH,
         ).wait_recv()
 
-    def whole(gat, slot, direction, hop):
-        if hop == 4:
-            return gat.at[slot, pl.ds(2 * direction, 2)]
-        return gat.at[slot]
-
     def mate_copy(which, gat, direction, hop, side_core):
-        part = whole(gat, 2 * origin(direction, hop) + side_core, direction, hop)
+        part = gat.at[2 * origin(direction, min(hop, 4)) + side_core]
+        if hop >= 4:
+            part = part.at[dict(arrivals(which, 4, hop - 4))[direction]]
         return pltpu.make_async_remote_copy(
             src_ref=part,
             dst_ref=part,
@@ -186,13 +183,11 @@
             device_id_type=MESH,
         )
 
-    def arrivals(hop, k):
+    def arrivals(which, hop, k):
+        order = ORDERS[which]
         if hop == 4:
-            return [(0, 1 - k), (1, 2 + k)]
-        return [(0, ORDER[k]), (1, ORDER[k])]
-
-    def steps(hop):
-        return range(2 if hop == 4 else H3)
+            return list(enumerate(sorted(order[2 * k : 2 * k + 2])))
+        return [(0, order[k]), (1, order[k])]
 
     sends = []
 
@@ -208,13 +203,15 @@
             go(mate_copy(which, gat, 0, 0, core))
 
     def ring_step(which, gat, hop, *ks):
-        last = [pair for k in range(2) for pair in arrivals(4, k)]
+        last = [pair for k in range(2) for pair in arrivals(which, 4, k)]
         for k in ks:
-            for direction, part in arrivals(hop, k):
+            for direction, part in arrivals(which, hop, k):
                 ring_wait(which, gat, direction, hop, part)
                 if hop < 3 or (hop == 3 and (direction, part) in last):
                     go(ring_copy(which, gat, direction, hop + 1, part))
-                if k == steps(hop)[-1]:
+                if hop == 4:
+                    go(mate_copy(which, gat, direction, 4 + k, core))
+                elif k == 3:
                     go(mate_copy(which, gat, direction, hop, core))
 
     def mate_step(which, gat, hop):
@@ -237,7 +234,7 @@
         jq = jq + jnp.sum(value * value, axis=0)
 
     pl.semaphore_wait(barrier, R - 1 + C - 1)
-    ring_start(0, gat1, ORDER)
+    ring_start(0, gat1, ORDERS[0])
     joined_sums = group_sums(js, jq, group_matrix(C3, 40, 0, 0), 64)
 
     loads["lat"].wait()
@@ -266,7 +263,7 @@
     ones1 = group_matrix(C1, 10, 0, 0)
     st_a1[0] = group_sums(ls, lq, ones1, 0) + joined_sums
     spread(st_a1, "rows", 0)
-    ring_step(0, gat1, 1, 0, 1)
+    ring_step(0, gat1, 1, 0, 1, 2)
 
     to_down.wait()
     to_up.wait()
@@ -295,14 +292,10 @@
     to_right.start()
     to_left.start()
 
-    ring_step(0, gat1, 1, 2, 3)
+    ring_step(0, gat1, 1, 3)
     st_a2[0] = collect(st_a1, "rows", 0)
     spread(st_a2, "cols", 1)
     ring_step(0, gat1, 2, 0, 1, 2, 3)
-    to_right.wait()
-    to_left.wait()
-    ring_step(0, gat1, 3, 0, 1)
-
     def group_rates(total):
         total = jnp.sum(total, axis=0, keepdims=True)
         total = jnp.broadcast_to(total, (8, 128))
@@ -352,8 +345,10 @@
                 live = live & (row < R - 1)
             put_row(i, value * scale1 + shift1, live)
 
+    to_right.wait()
+    to_left.wait()
     act1_rows(0, 20)
-    ring_step(0, gat1, 3, 2, 3)
+    ring_step(0, gat1, 3, 0, 1)
 
     def conv1(weights, first, count, width):
         total = None
@@ -363,42 +358,45 @@
             total = part if total is None else total + part
         return total.reshape(count, width, C1)
 
-    def norm3(slot):
-        for i in range(H3):
+    def norm3(slot, parts):
+        for i in parts:
             value = gat1[slot, i].astype(F32) * scale3 + shift3
             act3[slot, i] = halves(value).astype(BF16)
 
+    def norm_hop(which, gat, norm, hop):
+        mate_step(which, gat, hop)
+        parts = range(H3) if hop < 4 else ORDERS[which][2 * hop - 8 : 2 * hop - 6]
+        for direction in range(1 if hop == 0 or hop >= 4 else 2):
+            for k in range(2):
+                norm(2 * origin(direction, min(hop, 4)) + k, parts)
+
     def norm3_hop(hop):
-        mate_step(0, gat1, hop)
-        for direction in range(1 if hop in (0, 4) else 2):
-            for k in range(2):
-                norm3(2 * origin(direction, hop) + k)
+        norm_hop(0, gat1, norm3, hop)
 
     loads["w1a"].wait()
     hid[pl.ds(0, 6)] = conv1(w1a, 0, 6, WP)
+    ring_step(0, gat1, 3, 2, 3)
     scale3, shift3 = channel_rates(rates, group_matrix(C3, 40, 64, 1), flat(g3a), flat(b3a))
-    norm3_hop(0)
-    norm3_hop(1)
-    ring_step(0, gat1, 4, 0, 1)
     hid[pl.ds(6, 6)] = conv1(w1a, 6, 6, WP)
-    norm3_hop(2)
-    hid[pl.ds(12, 6)] = conv1(w1a, 12, 6, WP)
-
-    hs = jnp.zeros((8, C1), F32)
-    hq = jnp.zeros((8, C1), F32)
-    for i in range(H1):
-        value = hid[i + 1, 0:W1, :].reshape(8, 8, C1)
-        hs = hs + jnp.sum(value, axis=0)
-        hq = hq + jnp.sum(value * value, axis=0)
-    st_b1[0] = group_sums(hs, hq, ones1, 0)
-    spread(st_b1, "rows", 2)
-
-    norm3_hop(3)
-    norm3_hop(4)
-
-    def taps(weights, source, dims, rows_of):
-        for i in rows_of:
-            prod[i] = lax.dot_general(weights[...], source(i), dims, preferred_element_type=F32)
+    for hop in range(4):
+        norm3_hop(hop)
+
+    def taps(weights, source, dims, i, first, last):
+        prod[i, pl.ds(first, last - first), :] = lax.dot_general(
+            weights[pl.ds(first, last - first), :], source(i), dims, preferred_element_type=F32
+        )
+
+    BAND = 3 * OC
+
+    def border_taps(*args):
+        taps(*args, 0, 2 * BAND, 3 * BAND)
+        taps(*args, 3, 0, BAND)
+
+    def other_taps(*args):
+        for i in (1, 2):
+            taps(*args, i, 0, 3 * BAND)
+        taps(*args, 0, 0, 2 * BAND)
+        taps(*args, 3, BAND, 3 * BAND)
 
     lane3 = iota((OC, W3), 1)
 
@@ -430,22 +428,27 @@
         ]
 
     def edges_out(which):
-        edge_s[which, 0] = combine(H3)
-        edge_s[which, 1] = combine(-1)
+        edge_s[which, 0] = combine(H3).astype(BF16)
+        edge_s[which, 1] = combine(-1).astype(BF16)
         copies = edge_copies(which)
         for copy in copies:
             copy.start()
         return copies
 
     def edges_in(which):
-        low = jnp.where(row > 0, edge_r[which, 0], 0.0)
-        high = jnp.where(row < R - 1, edge_r[which, 1], 0.0)
+        low = jnp.where(row > 0, edge_r[which, 0].astype(F32), 0.0)
+        high = jnp.where(row < R - 1, edge_r[which, 1].astype(F32), 0.0)
         return low, high
 
     loads["w3a"].wait()
-    taps(w3a, lambda i: act3[:, i].reshape(W3, C3), NT, (0, 3))
+    first3 = (w3a, lambda i: act3[:, i].reshape(W3, C3), NT)
+    ring_step(0, gat1, 4, 0)
+    norm3_hop(4)
+    border_taps(*first3)
     copies = edges_out(0)
-    taps(w3a, lambda i: act3[:, i].reshape(W3, C3), NT, (1, 2))
+    ring_step(0, gat1, 4, 1)
+    norm3_hop(5)
+    other_taps(*first3)
     for i in (1, 2):
         value = combine(i)
         hid3[i] = value
@@ -476,16 +479,17 @@
     st_c[0] = jnp.sum(laid.reshape(OC // 8, 8, 128), axis=0)
     spread(st_c, "rows", 4)
 
-    pick = jnp.where(iota((OC, C3), 1) == iota((OC, C3), 0) + col * OC, 1.0, 0.0).astype(BF16)
-
-    def residual(i, carry):
-        res[i] = lax.dot_general(pick, gat1[:, i].reshape(W3, C3), NT, preferred_element_type=F32)
-        return carry
-
-    lax.fori_loop(0, H3, residual, 0)
-    ring_step(1, gat2, 1, 0, 1)
-    st_b2[0] = collect(st_b1, "rows", 2)
-    spread(st_b2, "cols", 3)
+    hid[pl.ds(12, 6)] = conv1(w1a, 12, 6, WP)
+    hs = jnp.zeros((8, C1), F32)
+    hq = jnp.zeros((8, C1), F32)
+    for i in range(H1):
+        value = hid[i + 1, 0:W1, :].reshape(8, 8, C1)
+        hs = hs + jnp.sum(value, axis=0)
+        hq = hq + jnp.sum(value * value, axis=0)
+    st_b1[0] = group_sums(hs, hq, ones1, 0)
+    spread(st_b1, "rows", 2)
+
+    ring_step(1, gat2, 1, 0, 1, 2, 3)
 
     total = jnp.sum(collect(st_c, "rows", 4), axis=0, keepdims=True)
     total = jnp.broadcast_to(total, (OC, 128)) / COUNT3
@@ -505,8 +509,19 @@
     st_d[0] = jnp.where(iota((8, 128), 0) == 0, *as_rows)
     spread(st_d, "cols", 5)
 
-    ring_step(1, gat2, 1, 2, 3)
-    ring_step(1, gat2, 2, 0, 1, 2)
+    ring_step(1, gat2, 2, 0, 1)
+    st_b2[0] = collect(st_b1, "rows", 2)
+    spread(st_b2, "cols", 3)
+
+    pick = jnp.where(iota((OC, C3), 1) == iota((OC, C3), 0) + col * OC, 1.0, 0.0).astype(BF16)
+
+    def residual(i, carry):
+        res[i] = lax.dot_general(pick, gat1[:, i].reshape(W3, C3), NT, preferred_element_type=F32)
+        return carry
+
+    lax.fori_loop(0, H3, residual, 0)
+    ring_step(1, gat2, 2, 2, 3)
+
     rates = group_rates(collect(st_b2, "cols", 3))
     scale2, shift2 = channel_rates(rates, group_matrix(C1, 10, 0, 1), flat(g1b), flat(b1b))
     near_ok = (place < W1) | ((place == W1) & (col < C - 1)) | ((place == WP - 1) & (col > 0))
@@ -521,48 +536,42 @@
             put_row(i, hid[i] * scale2 + shift2, live)
 
     act2_rows(0, 18)
-    ring_step(1, gat2, 2, 3)
-    ring_step(1, gat2, 3, 0)
+    ring_step(1, gat2, 3, 0, 1)
     loads["w1b"].wait()
 
-    def norm4(slot):
+    def norm4(slot, parts):
         block = st_d[(col + C - slot) % C]
         scale, shift = (jnp.sum(jnp.where(eye, block[j : j + 1], 0.0), axis=1, keepdims=True) for j in range(2))
-        for i in range(H3):
+        for i in parts:
             act4[slot, i] = halves(gat2[slot, i].astype(F32) * scale + shift).astype(BF16)
 
     def norm4_hop(hop):
-        mate_step(1, gat2, hop)
-        for direction in range(1 if hop in (0, 4) else 2):
-            for k in range(2):
-                norm4(2 * origin(direction, hop) + k)
+        norm_hop(1, gat2, norm4, hop)
 
     def out1_rows(first, count):
         value = conv1(w1b, first, count, W1) + flat(c1b).reshape(1, 1, C1)
         o1[pl.ds(first, count)] = (lat[pl.ds(first, count)].astype(F32) + value).astype(BF16)
 
     out1_rows(0, 4)
+    ring_step(1, gat2, 3, 2, 3)
+    out1_rows(4, 4)
     arrived(st_d, "cols", 5)
-    norm4_hop(0)
-    ring_step(1, gat2, 3, 1, 2)
-    out1_rows(4, 4)
-    norm4_hop(1)
-    ring_step(1, gat2, 3, 3)
+    for hop in range(4):
+        norm4_hop(hop)
+    loads["w3b"].wait()
+    second3 = (w3b, lambda i: act4[:, i].reshape(C3, W3), (((1,), (0,)), ((), ())))
+    bias3 = upright(c3b)
     out1_rows(8, 4)
     ring_step(1, gat2, 4, 0)
+    norm4_hop(4)
+    ring_step(1, gat2, 4, 1)
+    norm4_hop(5)
+    border_taps(*second3)
+    copies = edges_out(1)
+    other_taps(*second3)
     out1_rows(12, 4)
     write1 = local(o1, out1_h, 7)
     write1.start()
-    ring_step(1, gat2, 4, 1)
-    bias3 = upright(c3b)
-    norm4_hop(2)
-    norm4_hop(3)
-    norm4_hop(4)
-
-    loads["w3b"].wait()
-    taps(w3b, lambda i: act4[:, i].reshape(C3, W3), (((1,), (0,)), ((), ())), (0, 3))
-    copies = edges_out(1)
-    taps(w3b, lambda i: act4[:, i].reshape(C3, W3), (((1,), (0,)), ((), ())), (1, 2))
     for i in range(H3):
         res[i] = res[i] + combine(i) + bias3
     for copy in copies:
@@ -625,8 +634,8 @@
             pltpu.VMEM((C, H3, 16, C3), BF16),
             pltpu.VMEM((C, H3, OC, W3), BF16),
             pltpu.VMEM((H3, 9 * OC, W3), F32),
-            pltpu.VMEM((2, 2, OC, W3), F32),
-            pltpu.VMEM((2, 2, OC, W3), F32),
+            pltpu.VMEM((2, 2, OC, W3), BF16),
+            pltpu.VMEM((2, 2, OC, W3), BF16),
             pltpu.VMEM((H3, OC, W3), F32),
             pltpu.VMEM((H3, OC, W3), F32),
             pltpu.VMEM((H1, W1, C1), BF16),
@@ -643,8 +652,8 @@
             pltpu.SemaphoreType.DMA((6,)),
             pltpu.SemaphoreType.DMA((2, 2, 4, 4)),
             pltpu.SemaphoreType.DMA((2, 2, 4, 4)),
-            pltpu.SemaphoreType.DMA((2, 2, 5)),
-            pltpu.SemaphoreType.DMA((2, 2, 5)),
+            pltpu.SemaphoreType.DMA((2, 2, 6)),
+            pltpu.SemaphoreType.DMA((2, 2, 6)),
             pltpu.SemaphoreType.DMA((4,)),
             pltpu.SemaphoreType.DMA((4,)),
             pltpu.SemaphoreType.DMA((2, 2)),

time: 74.5 us -> 71.3 us (0.957)
  Pallas kernels: 70 us -> 66.9 us
    pallas_call x1, Pallas kernels: 70 us -> 66.9 us  [body(): pl.pallas_call(kernel, out_shape=(jax.ShapeDtypeStruct((H1, W1, C1), BF16...]
where the time goes in v4:
time: 71.3 us; the launch traced here: 71.2 us
  Pallas kernels  66.9 us (94%)
  local copies, waits for them, and re-layouts  3.68 us (5%)
    pallas_call x1, Pallas kernels, body(): pl.pallas_call(kernel, out_shape=(jax.ShapeDtypeStruct((H1, W1, C1), BF16...  66.9 us
    unnamed x2, local copies, waits for them, and re-layouts  3.68 us

profile of v4, /device:TPU:1, one launch (start us, length us, event | category | flops | bytes accessed | tf_op | source)
XLA Modules:
  0.0 71.2 jit_solution(1349694005666081358)
XLA Ops:
  0.6 66.9 %shard_map.176 = (bf16[16,64,320]{2,1,0:T(8,128)(2,1)}, bf16[4,80,256]{2,1,0:T(8,128)(2,1)}) custom-call(bf16[16,64,320]{2,1,0:T(8,128)(2,1)} %lat_h.1, f32[320]{0:T(512)} %g1a_h.1, f32[320]{0:T(512)} %b1a_h.1, bf16[3,960,320]{2,1,0:T(8,128)(2,1)} %bitcast.9, f32[320]{0:T(512)} %g1b_h.1, f32[320]{0:T(512)} %b1b_h.1, bf16[3,960,320]{2,1,0:T(8,128)(2,1)} %bitcast.10, ...), custom_call_target="tpu_custom_call" | custom-call | tf_op jit(solution)/shard_map/pallas_call | solution.py:610
  67.5 2.1 %copy.21 = bf16[16,64,320]{2,1,0:T(8,128)(2,1)} copy(bf16[16,64,320]{2,1,0:T(8,128)(2,1)} %get-tuple-element.8) | data formatting | bytes 1310720
  69.6 1.6 %copy.22 = bf16[4,256,80]{1,2,0:T(8,128)(2,1)} copy(bf16[4,256,80]{1,2,0:T(8,128)(2,1)} %bitcast.13) | data formatting | bytes 327680

commit v5 on v4

--- a/solution.py
+++ b/solution.py
@@ -587,6 +587,20 @@
         copy.wait_send()
     write1.wait()
     write3.wait()
+
+
+def deliver(from1, from3, to1, to3, held1, held3, load_sem, store_sem):
+    pieces = [(from3, held3, to3)]
+    pieces += [tuple(x.at[pl.ds(4 * i, 4)] for x in (from1, held1, to1)) for i in range(H1 // 4)]
+    loads = [pltpu.make_async_copy(a, b, load_sem.at[i]) for i, (a, b, _) in enumerate(pieces)]
+    stores = [pltpu.make_async_copy(b, c, store_sem.at[i]) for i, (_, b, c) in enumerate(pieces)]
+    for copy in loads:
+        copy.start()
+    for load, store in zip(loads, stores):
+        load.wait()
+        store.start()
+    for copy in stores:
+        copy.wait()
 
 
 def body(
@@ -663,6 +677,21 @@
             collective_id=0, has_side_effects=True, vmem_limit_bytes=56 * 1024 * 1024
         ),
     )(*[value for value, _ in operands])
+    out1, out3 = pl.pallas_call(
+        deliver,
+        out_shape=(
+            jax.ShapeDtypeStruct((H1, W1, C1), BF16),
+            jax.ShapeDtypeStruct((H3, OC, W3), BF16),
+        ),
+        in_specs=[any_spec, any_spec],
+        out_specs=(any_spec, any_spec),
+        scratch_shapes=[
+            pltpu.VMEM((H1, W1, C1), BF16),
+            pltpu.VMEM((H3, OC, W3), BF16),
+            pltpu.SemaphoreType.DMA((5,)),
+            pltpu.SemaphoreType.DMA((5,)),
+        ],
+    )(out1, out3)
     return out1, jnp.swapaxes(out3, 1, 2)
 
 

time: 71.3 us -> 69.8 us (0.979)
  local copies, waits for them, and re-layouts: 3.68 us -> 0 us
  Pallas kernels: 66.9 us -> 68.9 us
    unnamed x2 -> x0, local copies, waits for them, and re-layouts: 3.68 us -> none
    pallas_call x0 -> x1, Pallas kernels: none -> 2.03 us  [body(): pl.pallas_call(deliver, out_shape=(jax.ShapeDtypeStruct((H1, W1, C1), BF1...]
where the time goes in v5:
time: 69.8 us; the launch traced here: 69.7 us
  Pallas kernels  68.9 us (99%)
  between operations  0.81 us (1%)
    pallas_call x1, Pallas kernels, body(): pl.pallas_call(kernel, out_shape=(jax.ShapeDtypeStruct((H1, W1, C1), BF16...  66.9 us
    pallas_call x1, Pallas kernels, body(): pl.pallas_call(deliver, out_shape=(jax.ShapeDtypeStruct((H1, W1, C1), BF1...  2.03 us

profile of v5, /device:TPU:1, one launch (start us, length us, event | category | flops | bytes accessed | tf_op | source)
XLA Modules:
  0.0 69.7 jit_solution(10346773823782013097)
XLA Ops:
  0.6 66.9 %shard_map.176 = (bf16[16,64,320]{2,1,0:T(8,128)(2,1)}, bf16[4,80,256]{2,1,0:T(8,128)(2,1)}) custom-call(bf16[16,64,320]{2,1,0:T(8,128)(2,1)} %lat_h.1, f32[320]{0:T(512)} %g1a_h.1, f32[320]{0:T(512)} %b1a_h.1, bf16[3,960,320]{2,1,0:T(8,128)(2,1)} %bitcast.9, f32[320]{0:T(512)} %g1b_h.1, f32[320]{0:T(512)} %b1b_h.1, bf16[3,960,320]{2,1,0:T(8,128)(2,1)} %bitcast.10, ...), custom_call_target="tpu_custom_call" | custom-call | tf_op jit(solution)/shard_map/pallas_call | solution.py:624
  67.5 2.0 %shard_map.177 = (bf16[16,64,320]{2,1,0:T(8,128)(2,1)}, bf16[4,80,256]{2,1,0:T(8,128)(2,1)}) custom-call(bf16[16,64,320]{2,1,0:T(8,128)(2,1)} %get-tuple-element.6.from1, bf16[4,80,256]{2,1,0:T(8,128)(2,1)} %get-tuple-element.7.from3), custom_call_target="tpu_custom_call" | custom-call | tf_op jit(solution)/shard_map/pallas_call | solution.py:680

commit v6 on v5

--- a/solution.py
+++ b/solution.py
@@ -522,6 +522,19 @@
     lax.fori_loop(0, H3, residual, 0)
     ring_step(1, gat2, 2, 2, 3)
 
+    def norm4(slot, parts):
+        block = st_d[(col + C - slot) % C]
+        scale, shift = (jnp.sum(jnp.where(eye, block[j : j + 1], 0.0), axis=1, keepdims=True) for j in range(2))
+        for i in parts:
+            act4[slot, i] = halves(gat2[slot, i].astype(F32) * scale + shift).astype(BF16)
+
+    def norm4_hop(hop):
+        norm_hop(1, gat2, norm4, hop)
+
+    arrived(st_d, "cols", 5)
+    norm4_hop(0)
+    norm4_hop(1)
+
     rates = group_rates(collect(st_b2, "cols", 3))
     scale2, shift2 = channel_rates(rates, group_matrix(C1, 10, 0, 1), flat(g1b), flat(b1b))
     near_ok = (place < W1) | ((place == W1) & (col < C - 1)) | ((place == WP - 1) & (col > 0))
@@ -539,15 +552,6 @@
     ring_step(1, gat2, 3, 0, 1)
     loads["w1b"].wait()
 
-    def norm4(slot, parts):
-        block = st_d[(col + C - slot) % C]
-        scale, shift = (jnp.sum(jnp.where(eye, block[j : j + 1], 0.0), axis=1, keepdims=True) for j in range(2))
-        for i in parts:
-            act4[slot, i] = halves(gat2[slot, i].astype(F32) * scale + shift).astype(BF16)
-
-    def norm4_hop(hop):
-        norm_hop(1, gat2, norm4, hop)
-
     def out1_rows(first, count):
         value = conv1(w1b, first, count, W1) + flat(c1b).reshape(1, 1, C1)
         o1[pl.ds(first, count)] = (lat[pl.ds(first, count)].astype(F32) + value).astype(BF16)
@@ -555,19 +559,18 @@
     out1_rows(0, 4)
     ring_step(1, gat2, 3, 2, 3)
     out1_rows(4, 4)
-    arrived(st_d, "cols", 5)
-    for hop in range(4):
-        norm4_hop(hop)
+    norm4_hop(2)
+    norm4_hop(3)
     loads["w3b"].wait()
     second3 = (w3b, lambda i: act4[:, i].reshape(C3, W3), (((1,), (0,)), ((), ())))
     bias3 = upright(c3b)
-    out1_rows(8, 4)
     ring_step(1, gat2, 4, 0)
     norm4_hop(4)
     ring_step(1, gat2, 4, 1)
     norm4_hop(5)
     border_taps(*second3)
     copies = edges_out(1)
+    out1_rows(8, 4)
     other_taps(*second3)
     out1_rows(12, 4)
     write1 = local(o1, out1_h, 7)

time: 69.8 us -> 68.8 us (0.986)
  Pallas kernels: 68.9 us -> 67.9 us
    pallas_call x1, Pallas kernels: 66.9 us -> 65.8 us  [body(): pl.pallas_call(kernel, out_shape=(jax.ShapeDtypeStruct((H1, W1, C1), BF16...]
where the time goes in v6:
time: 68.8 us; the launch traced here: 68.7 us
  Pallas kernels  67.9 us (99%)
  between operations  0.81 us (1%)
    pallas_call x1, Pallas kernels, body(): pl.pallas_call(kernel, out_shape=(jax.ShapeDtypeStruct((H1, W1, C1), BF16...  65.8 us
    pallas_call x1, Pallas kernels, body(): pl.pallas_call(deliver, out_shape=(jax.ShapeDtypeStruct((H1, W1, C1), BF1...  2.03 us

profile of v6, /device:TPU:1, one launch (start us, length us, event | category | flops | bytes accessed | tf_op | source)
XLA Modules:
  0.0 68.7 jit_solution(5314956032800758199)
XLA Ops:
  0.6 65.8 %shard_map.176 = (bf16[16,64,320]{2,1,0:T(8,128)(2,1)}, bf16[4,80,256]{2,1,0:T(8,128)(2,1)}) custom-call(bf16[16,64,320]{2,1,0:T(8,128)(2,1)} %lat_h.1, f32[320]{0:T(512)} %g1a_h.1, f32[320]{0:T(512)} %b1a_h.1, bf16[3,960,320]{2,1,0:T(8,128)(2,1)} %bitcast.9, f32[320]{0:T(512)} %g1b_h.1, f32[320]{0:T(512)} %b1b_h.1, bf16[3,960,320]{2,1,0:T(8,128)(2,1)} %bitcast.10, ...), custom_call_target="tpu_custom_call" | custom-call | tf_op jit(solution)/shard_map/pallas_call | solution.py:627
  66.5 2.0 %shard_map.177 = (bf16[16,64,320]{2,1,0:T(8,128)(2,1)}, bf16[4,80,256]{2,1,0:T(8,128)(2,1)}) custom-call(bf16[16,64,320]{2,1,0:T(8,128)(2,1)} %get-tuple-element.6.from1, bf16[4,80,256]{2,1,0:T(8,128)(2,1)} %get-tuple-element.7.from3), custom_call_target="tpu_custom_call" | custom-call | tf_op jit(solution)/shard_map/pallas_call | solution.py:683

commit v7 on v6

--- a/solution.py
+++ b/solution.py
@@ -509,9 +509,9 @@
     st_d[0] = jnp.where(iota((8, 128), 0) == 0, *as_rows)
     spread(st_d, "cols", 5)
 
-    ring_step(1, gat2, 2, 0, 1)
     st_b2[0] = collect(st_b1, "rows", 2)
     spread(st_b2, "cols", 3)
+    ring_step(1, gat2, 2, 0, 1)
 
     pick = jnp.where(iota((OC, C3), 1) == iota((OC, C3), 0) + col * OC, 1.0, 0.0).astype(BF16)
 

time: 68.8 us -> 67.1 us (0.975)
  Pallas kernels: 67.9 us -> 66.2 us
    pallas_call x1, Pallas kernels: 65.8 us -> 64.2 us  [body(): pl.pallas_call(kernel, out_shape=(jax.ShapeDtypeStruct((H1, W1, C1), BF16...]
where the time goes in v7:
time: 67.1 us; the launch traced here: 67 us
  Pallas kernels  66.2 us (99%)
  between operations  0.81 us (1%)
    pallas_call x1, Pallas kernels, body(): pl.pallas_call(kernel, out_shape=(jax.ShapeDtypeStruct((H1, W1, C1), BF16...  64.2 us
    pallas_call x1, Pallas kernels, body(): pl.pallas_call(deliver, out_shape=(jax.ShapeDtypeStruct((H1, W1, C1), BF1...  2.03 us

profile of v7, /device:TPU:1, one launch (start us, length us, event | category | flops | bytes accessed | tf_op | source)
XLA Modules:
  0.0 67.0 jit_solution(16626107912991566693)
XLA Ops:
  0.6 64.2 %shard_map.176 = (bf16[16,64,320]{2,1,0:T(8,128)(2,1)}, bf16[4,80,256]{2,1,0:T(8,128)(2,1)}) custom-call(bf16[16,64,320]{2,1,0:T(8,128)(2,1)} %lat_h.1, f32[320]{0:T(512)} %g1a_h.1, f32[320]{0:T(512)} %b1a_h.1, bf16[3,960,320]{2,1,0:T(8,128)(2,1)} %bitcast.9, f32[320]{0:T(512)} %g1b_h.1, f32[320]{0:T(512)} %b1b_h.1, bf16[3,960,320]{2,1,0:T(8,128)(2,1)} %bitcast.10, ...), custom_call_target="tpu_custom_call" | custom-call | tf_op jit(solution)/shard_map/pallas_call | solution.py:627
  64.8 2.0 %shard_map.177 = (bf16[16,64,320]{2,1,0:T(8,128)(2,1)}, bf16[4,80,256]{2,1,0:T(8,128)(2,1)}) custom-call(bf16[16,64,320]{2,1,0:T(8,128)(2,1)} %get-tuple-element.6.from1, bf16[4,80,256]{2,1,0:T(8,128)(2,1)} %get-tuple-element.7.from3), custom_call_target="tpu_custom_call" | custom-call | tf_op jit(solution)/shard_map/pallas_call | solution.py:683

commit v8 on v7

--- a/solution.py
+++ b/solution.py
@@ -264,6 +264,8 @@
     st_a1[0] = group_sums(ls, lq, ones1, 0) + joined_sums
     spread(st_a1, "rows", 0)
     ring_step(0, gat1, 1, 0, 1, 2)
+    st_a2[0] = collect(st_a1, "rows", 0)
+    spread(st_a2, "cols", 1)
 
     to_down.wait()
     to_up.wait()
@@ -293,8 +295,6 @@
     to_left.start()
 
     ring_step(0, gat1, 1, 3)
-    st_a2[0] = collect(st_a1, "rows", 0)
-    spread(st_a2, "cols", 1)
     ring_step(0, gat1, 2, 0, 1, 2, 3)
     def group_rates(total):
         total = jnp.sum(total, axis=0, keepdims=True)

time: 67.1 us -> 66.3 us (0.988)
  Pallas kernels: 66.2 us -> 65.3 us
    pallas_call x1, Pallas kernels: 64.2 us -> 63.3 us  [body(): pl.pallas_call(kernel, out_shape=(jax.ShapeDtypeStruct((H1, W1, C1), BF16...]
where the time goes in v8:
time: 66.3 us; the launch traced here: 66.1 us
  Pallas kernels  65.3 us (98%)
  between operations  0.81 us (1%)
    pallas_call x1, Pallas kernels, body(): pl.pallas_call(kernel, out_shape=(jax.ShapeDtypeStruct((H1, W1, C1), BF16...  63.3 us
    pallas_call x1, Pallas kernels, body(): pl.pallas_call(deliver, out_shape=(jax.ShapeDtypeStruct((H1, W1, C1), BF1...  2.03 us

profile of v8, /device:TPU:1, one launch (start us, length us, event | category | flops | bytes accessed | tf_op | source)
XLA Modules:
  0.0 66.1 jit_solution(8865464932503647684)
XLA Ops:
  0.6 63.3 %shard_map.176 = (bf16[16,64,320]{2,1,0:T(8,128)(2,1)}, bf16[4,80,256]{2,1,0:T(8,128)(2,1)}) custom-call(bf16[16,64,320]{2,1,0:T(8,128)(2,1)} %lat_h.1, f32[320]{0:T(512)} %g1a_h.1, f32[320]{0:T(512)} %b1a_h.1, bf16[3,960,320]{2,1,0:T(8,128)(2,1)} %bitcast.9, f32[320]{0:T(512)} %g1b_h.1, f32[320]{0:T(512)} %b1b_h.1, bf16[3,960,320]{2,1,0:T(8,128)(2,1)} %bitcast.10, ...), custom_call_target="tpu_custom_call" | custom-call | tf_op jit(solution)/shard_map/pallas_call | solution.py:627
  63.9 2.0 %shard_map.177 = (bf16[16,64,320]{2,1,0:T(8,128)(2,1)}, bf16[4,80,256]{2,1,0:T(8,128)(2,1)}) custom-call(bf16[16,64,320]{2,1,0:T(8,128)(2,1)} %get-tuple-element.6.from1, bf16[4,80,256]{2,1,0:T(8,128)(2,1)} %get-tuple-element.7.from3), custom_call_target="tpu_custom_call" | custom-call | tf_op jit(solution)/shard_map/pallas_call | solution.py:683
